TPU v7x, 32 devices: a whole 2x2x4 slice. The times are simulated.
32 devices in a mesh: src: 4 (over y, core), vocab: 8 (over z, x).
Axes of the slice: x: 2, y: 2, z: 4, core: 2. Of those that a mesh axis runs over, the one named last changes fastest.
Arguments:
- queries: bfloat16 [2048, 2048], P('vocab', 'src'), may hold values from -35 to 35
- enc_keys: bfloat16 [8, 256, 2048], P('vocab', None, 'src'), may hold values from -4 to 4
- enc_values: bfloat16 [8, 256, 2048], P('vocab', None, 'src'), may hold values from -48 to 48
- source_lengths: int32 [8], P('vocab'), may hold values from 1 to 256, 1024 in all
- out_proj: bfloat16 [2048, 2048], P('src'), may hold values from -0.125 to 0.125
- dec_state: bfloat16 [2048, 2048], P('vocab', 'src'), may hold values from -24 to 24
- norm_gain: float32 [2048], P('src'), may hold values from 0.25 to 1.75
- norm_bias: float32 [2048], P('src'), may hold values from -3 to 3
- head_weight: bfloat16 [2048, 64512], P('src', 'vocab'), may hold values from -2 to 2
- shortlist: int32 [2048, 8], P('vocab'), may hold values from 0 to 503, all different within a row; in each aligned block of 256 rows (0 to 255, 256 to 511, ...) at most 8 rows name the same one
- target_slot: int32 [2048], P('vocab'), may hold values from 0 to 7
- target_offset: int32 [2048], P('vocab'), may hold values from 0 to 127
Outputs:
- row_loss: float32 [2048], P('vocab')
- grad_state: float32 [2048, 2048], P('vocab', 'src')
Inputs may be any that keep to these rules, and one draw needn't show every extreme that they name: `shortlist`: each row lists 8 different blocks; the rows of one sentence list one block at most 8 times.
All inputs are finite; a program needn't handle non-finite values. No bound on the sum of `source_lengths` on one device may be relied on, other than what follows from the above.
Results may differ from a plain program's by a relative error of at most 0.0055.
Values may be sent and summed in bfloat16 or wider, within the bound.
A program may use at most 64 MiB of HBM per device.

v0:
```python
import math

import jax
import jax.numpy as jnp
from jax import lax
from jax.sharding import PartitionSpec as P

HD = 128
BLK = 128


MASKED = -1e30
EPSILON = 1e-05


def slot_stats(full_logits, code_grid):
    slot_top = jnp.max(full_logits, axis=-1)
    slot_spread = jnp.sum(jnp.exp(full_logits - slot_top[..., None]), axis=-1)
    offsets = lax.broadcasted_iota(jnp.int32, full_logits.shape, 3)
    slot_pick = jnp.sum(jnp.where(offsets == code_grid[..., None], full_logits, 0.0), axis=-1)
    return (slot_top, slot_spread, slot_pick)


def slot_delta(full_logits, row_totals, code_grid):
    offsets = lax.broadcasted_iota(jnp.int32, full_logits.shape, 3)
    target_hit = (offsets == code_grid[..., None]).astype(jnp.float32)
    return (jnp.exp(full_logits - row_totals[..., None]) - target_hit).astype(jnp.bfloat16)


def shards(
    queries,
    enc_keys,
    enc_values,
    source_lengths,
    out_proj,
    dec_state,
    norm_gain,
    norm_bias,
    head_weight,
    shortlist,
    target_slot,
    target_offset,
):
    voc_count = lax.axis_size("vocab")
    row_count = queries.shape[0]
    mem_count = enc_keys.shape[1]
    model_width = out_proj.shape[1]
    width_dev = dec_state.shape[1]
    heads_dev = enc_keys.shape[2] // HD
    q_heads = queries.reshape(row_count, heads_dev, HD)
    key_heads = enc_keys[0].reshape(mem_count, heads_dev, HD)
    value_heads = enc_values[0].reshape(mem_count, heads_dev, HD)
    scores = jnp.einsum("rhe,phe->hrp", q_heads, key_heads, preferred_element_type=jnp.float32) * (
        1.0 / math.sqrt(HD)
    )
    positions = lax.iota(jnp.int32, mem_count)
    usable = (positions < source_lengths[0])[None, None, :]
    scores = jnp.where(usable, scores, MASKED)
    row_top = jnp.max(scores, axis=-1)
    raw_weights = jnp.where(usable, jnp.exp(scores - row_top[..., None]), 0.0)
    totals = jnp.sum(raw_weights, axis=-1)
    mixture = jnp.einsum(
        "hrp,phe->rhe",
        raw_weights.astype(jnp.bfloat16),
        value_heads,
        preferred_element_type=jnp.float32,
    )
    own_mix = mixture / totals.T[..., None]
    attn_own = own_mix.astype(jnp.bfloat16).reshape(row_count, heads_dev * HD)
    projected = lax.psum_scatter(
        lax.dot_general(
            out_proj, attn_own, (((0,), (1,)), ((), ())), preferred_element_type=jnp.float32
        ),
        "src",
        scatter_dimension=0,
        tiled=True,
    )
    residual = dec_state.astype(jnp.float32) + projected.T
    sum_rows, square_rows = lax.psum(
        (jnp.sum(residual, axis=1), jnp.sum(residual * residual, axis=1)), "src"
    )
    row_mean = sum_rows / model_width
    variance = square_rows / model_width - row_mean * row_mean
    inv_std = lax.rsqrt(variance + EPSILON)
    centered = (residual - row_mean[:, None]) * inv_std[:, None]
    normed = (centered * norm_gain + norm_bias).astype(jnp.bfloat16)
    list_count = shortlist.shape[1]
    blocks_dev = head_weight.shape[1] // BLK
    vocab_blocks = blocks_dev * voc_count
    bucket_most = max(2, 2 * row_count * list_count // vocab_blocks)
    slot_total = vocab_blocks * bucket_most
    pair_count = row_count * list_count
    listed = shortlist.reshape(pair_count)
    sort_order = jnp.argsort(listed, stable=True)
    sorted_ids = listed[sort_order]
    firsts = jnp.searchsorted(sorted_ids, sorted_ids, side="left")
    slot_ranks = (
        jnp.zeros((pair_count,), jnp.int32)
        .at[sort_order]
        .set(jnp.arange(pair_count, dtype=jnp.int32) - firsts)
    )
    slot_ids = listed * bucket_most + slot_ranks
    pair_rows = jnp.arange(pair_count, dtype=jnp.int32) // list_count
    pair_lists = jnp.arange(pair_count, dtype=jnp.int32) % list_count
    outgoing = jnp.zeros((slot_total, width_dev), jnp.bfloat16).at[slot_ids].set(normed[pair_rows])
    is_target = pair_lists == target_slot[pair_rows]
    target_codes = (
        jnp.full((slot_total,), -2, jnp.int32)
        .at[slot_ids]
        .set(jnp.where(is_target, target_offset[pair_rows], -1))
    )
    incoming = lax.all_to_all(
        outgoing.reshape(voc_count, blocks_dev * bucket_most, width_dev),
        "vocab",
        split_axis=0,
        concat_axis=0,
        tiled=True,
    )
    in_codes = lax.all_to_all(
        target_codes.reshape(voc_count, blocks_dev * bucket_most),
        "vocab",
        split_axis=0,
        concat_axis=0,
        tiled=True,
    )
    received = incoming.reshape(voc_count, blocks_dev, bucket_most, width_dev)
    code_grid = in_codes.reshape(voc_count, blocks_dev, bucket_most)
    weight_view = head_weight.reshape(width_dev, blocks_dev, BLK)
    partial_logits = jnp.einsum(
        "slmd,dlt->slmt", received, weight_view, preferred_element_type=jnp.float32
    )
    full_logits = lax.psum(partial_logits, "src")
    slot_top, slot_spread, slot_pick = slot_stats(full_logits, code_grid)
    back_top, back_spread, back_pick = (
        lax.all_to_all(
            slot_top.reshape(voc_count, blocks_dev * bucket_most),
            "vocab",
            split_axis=0,
            concat_axis=0,
            tiled=True,
        ),
        lax.all_to_all(
            slot_spread.reshape(voc_count, blocks_dev * bucket_most),
            "vocab",
            split_axis=0,
            concat_axis=0,
            tiled=True,
        ),
        lax.all_to_all(
            slot_pick.reshape(voc_count, blocks_dev * bucket_most),
            "vocab",
            split_axis=0,
            concat_axis=0,
            tiled=True,
        ),
    )
    pair_top = back_top.reshape(slot_total)[slot_ids].reshape(row_count, list_count)
    pair_spread = back_spread.reshape(slot_total)[slot_ids].reshape(row_count, list_count)
    pair_pick = back_pick.reshape(slot_total)[slot_ids].reshape(row_count, list_count)
    row_best = jnp.max(pair_top, axis=1)
    log_total = row_best + jnp.log(
        jnp.sum(jnp.exp(pair_top - row_best[:, None]) * pair_spread, axis=1)
    )
    list_iota = lax.broadcasted_iota(jnp.int32, (row_count, list_count), 1)
    target_logit = jnp.sum(jnp.where(list_iota == target_slot[:, None], pair_pick, 0.0), axis=1)
    row_loss = log_total - target_logit
    total_out = jnp.zeros((slot_total,), jnp.float32).at[slot_ids].set(log_total[pair_rows])
    total_in = lax.all_to_all(
        total_out.reshape(voc_count, blocks_dev * bucket_most),
        "vocab",
        split_axis=0,
        concat_axis=0,
        tiled=True,
    )
    total_in = total_in.reshape(voc_count, blocks_dev, bucket_most)
    deltas = slot_delta(full_logits, total_in, code_grid)
    grad_slots = jnp.einsum(
        "slmt,dlt->slmd", deltas, weight_view, preferred_element_type=jnp.float32
    )
    returned = lax.all_to_all(
        grad_slots.reshape(voc_count, blocks_dev * bucket_most, width_dev).astype(jnp.bfloat16),
        "vocab",
        split_axis=0,
        concat_axis=0,
        tiled=True,
    ).astype(jnp.float32)
    returned = returned.reshape(slot_total, width_dev)
    grad_normed = jnp.sum(returned[slot_ids].reshape(row_count, list_count, width_dev), axis=1)
    gained = grad_normed * norm_gain
    sum_g, sum_gx = lax.psum((jnp.sum(gained, axis=1), jnp.sum(gained * centered, axis=1)), "src")
    grad_state = inv_std[:, None] * (
        gained - (sum_g / model_width)[:, None] - centered * (sum_gx / model_width)[:, None]
    )
    return (row_loss, grad_state)


def solution(mesh):
    placed = (
        P("vocab", "src"),
        P("vocab", None, "src"),
        P("vocab", None, "src"),
        P("vocab"),
        P("src", None),
        P("vocab", "src"),
        P("src"),
        P("src"),
        P("src", "vocab"),
        P("vocab", None),
        P("vocab"),
        P("vocab"),
    )
    return jax.shard_map(
        shards,
        mesh=mesh,
        in_specs=placed,
        out_specs=(P("vocab"), P("vocab", "src")),
        check_vma=False,
    )
```

profile of v0, /device:TPU:11, one launch (start us, length us, event | category | flops | bytes accessed | tf_op | source)
XLA Modules:
  0.0 602.3 jit_solution(5892449344732483127)
XLA Ops:
  8.0 1.0 reshape_squeeze.6
  9.0 1.5 fusion.42
  10.5 1.2 fusion.12
  11.8 1.8 copy.54
  13.6 1.3 fusion.14
  14.9 2.1 convolution_bitcast_fusion
  17.3 5.0 sort.17
  22.4 11.8 %gather_fusion.1 = s32[2048]{0:T(1024)S(1)} fusion(s32[2048]{0:T(1024)S(1)} %reshape.136, s32[2048]{0:T(1024)S(1)} %get-tuple-element.111), kind=kCustom, calls=%fused_computation.1 | custom fusion | bytes 24576 | tf_op jit(solution)/shard_map/gather | solution.py:95
  34.2 142.4 %while.25 = (s32[]{:T(128)}, u32[2048]{0:T(1024)S(1)}, u32[2048]{0:T(1024)S(1)}, s32[2048]{0:T(1024)S(1)}, s32[]{:T(128)}, /*index=5*/s32[]{:T(128)}, s32[]{}) while((s32[]{:T(128)}, u32[2048]{0:T(1024)S(1)}, u32[2048]{0:T(1024)S(1)}, s32[2048]{0:T(1024)S(1)}, s32[]{:T(128)}, /*index=5*/s32[]{:T(128)}, s32[]{}) %tuple.48), condition=%wide.region_2.3_spmd.clone, body=%wide.region_1.2_spmd.clone.sunk | while | flops 38916 | bytes 135269 | solution.py:96
  34.2 11.8 %gather_fusion = s32[2048]{0:T(1024)S(1)} fusion(s32[2048]{0:T(1024)S(1)} %get-tuple-element.162, u32[2048]{0:T(1024)S(1)} %broadcast_clamp_fusion.5), kind=kCustom, calls=%fused_computation.clone.clone.1 | custom fusion | bytes 24576 | tf_op jit(solution)/shard_map/jit(searchsorted)/jit(_searchsorted_scan_impl)/vmap(jit(_searchsorted_scan_impl))/while/body/eval_jaxpr/gather | solution.py:96
  46.1 11.8 %gather_fusion = s32[2048]{0:T(1024)S(1)} fusion(s32[2048]{0:T(1024)S(1)} %get-tuple-element.162, u32[2048]{0:T(1024)S(1)} %broadcast_clamp_fusion.5), kind=kCustom, calls=%fused_computation.clone.clone.1 | custom fusion | bytes 24576 | tf_op jit(solution)/shard_map/jit(searchsorted)/jit(_searchsorted_scan_impl)/vmap(jit(_searchsorted_scan_impl))/while/body/eval_jaxpr/gather | solution.py:96
  58.0 11.8 %gather_fusion = s32[2048]{0:T(1024)S(1)} fusion(s32[2048]{0:T(1024)S(1)} %get-tuple-element.162, u32[2048]{0:T(1024)S(1)} %broadcast_clamp_fusion.5), kind=kCustom, calls=%fused_computation.clone.clone.1 | custom fusion | bytes 24576 | tf_op jit(solution)/shard_map/jit(searchsorted)/jit(_searchsorted_scan_impl)/vmap(jit(_searchsorted_scan_impl))/while/body/eval_jaxpr/gather | solution.py:96
  69.8 11.8 %gather_fusion = s32[2048]{0:T(1024)S(1)} fusion(s32[2048]{0:T(1024)S(1)} %get-tuple-element.162, u32[2048]{0:T(1024)S(1)} %broadcast_clamp_fusion.5), kind=kCustom, calls=%fused_computation.clone.clone.1 | custom fusion | bytes 24576 | tf_op jit(solution)/shard_map/jit(searchsorted)/jit(_searchsorted_scan_impl)/vmap(jit(_searchsorted_scan_impl))/while/body/eval_jaxpr/gather | solution.py:96
  81.7 11.8 %gather_fusion = s32[2048]{0:T(1024)S(1)} fusion(s32[2048]{0:T(1024)S(1)} %get-tuple-element.162, u32[2048]{0:T(1024)S(1)} %broadcast_clamp_fusion.5), kind=kCustom, calls=%fused_computation.clone.clone.1 | custom fusion | bytes 24576 | tf_op jit(solution)/shard_map/jit(searchsorted)/jit(_searchsorted_scan_impl)/vmap(jit(_searchsorted_scan_impl))/while/body/eval_jaxpr/gather | solution.py:96
  93.6 11.8 %gather_fusion = s32[2048]{0:T(1024)S(1)} fusion(s32[2048]{0:T(1024)S(1)} %get-tuple-element.162, u32[2048]{0:T(1024)S(1)} %broadcast_clamp_fusion.5), kind=kCustom, calls=%fused_computation.clone.clone.1 | custom fusion | bytes 24576 | tf_op jit(solution)/shard_map/jit(searchsorted)/jit(_searchsorted_scan_impl)/vmap(jit(_searchsorted_scan_impl))/while/body/eval_jaxpr/gather | solution.py:96
  105.4 11.8 %gather_fusion = s32[2048]{0:T(1024)S(1)} fusion(s32[2048]{0:T(1024)S(1)} %get-tuple-element.162, u32[2048]{0:T(1024)S(1)} %broadcast_clamp_fusion.5), kind=kCustom, calls=%fused_computation.clone.clone.1 | custom fusion | bytes 24576 | tf_op jit(solution)/shard_map/jit(searchsorted)/jit(_searchsorted_scan_impl)/vmap(jit(_searchsorted_scan_impl))/while/body/eval_jaxpr/gather | solution.py:96
  117.3 11.8 %gather_fusion = s32[2048]{0:T(1024)S(1)} fusion(s32[2048]{0:T(1024)S(1)} %get-tuple-element.162, u32[2048]{0:T(1024)S(1)} %broadcast_clamp_fusion.5), kind=kCustom, calls=%fused_computation.clone.clone.1 | custom fusion | bytes 24576 | tf_op jit(solution)/shard_map/jit(searchsorted)/jit(_searchsorted_scan_impl)/vmap(jit(_searchsorted_scan_impl))/while/body/eval_jaxpr/gather | solution.py:96
  129.2 11.8 %gather_fusion = s32[2048]{0:T(1024)S(1)} fusion(s32[2048]{0:T(1024)S(1)} %get-tuple-element.162, u32[2048]{0:T(1024)S(1)} %broadcast_clamp_fusion.5), kind=kCustom, calls=%fused_computation.clone.clone.1 | custom fusion | bytes 24576 | tf_op jit(solution)/shard_map/jit(searchsorted)/jit(_searchsorted_scan_impl)/vmap(jit(_searchsorted_scan_impl))/while/body/eval_jaxpr/gather | solution.py:96
  141.0 11.8 %gather_fusion = s32[2048]{0:T(1024)S(1)} fusion(s32[2048]{0:T(1024)S(1)} %get-tuple-element.162, u32[2048]{0:T(1024)S(1)} %broadcast_clamp_fusion.5), kind=kCustom, calls=%fused_computation.clone.clone.1 | custom fusion | bytes 24576 | tf_op jit(solution)/shard_map/jit(searchsorted)/jit(_searchsorted_scan_impl)/vmap(jit(_searchsorted_scan_impl))/while/body/eval_jaxpr/gather | solution.py:96
  152.9 11.8 %gather_fusion = s32[2048]{0:T(1024)S(1)} fusion(s32[2048]{0:T(1024)S(1)} %get-tuple-element.162, u32[2048]{0:T(1024)S(1)} %broadcast_clamp_fusion.5), kind=kCustom, calls=%fused_computation.clone.clone.1 | custom fusion | bytes 24576 | tf_op jit(solution)/shard_map/jit(searchsorted)/jit(_searchsorted_scan_impl)/vmap(jit(_searchsorted_scan_impl))/while/body/eval_jaxpr/gather | solution.py:96
  164.8 11.8 %gather_fusion = s32[2048]{0:T(1024)S(1)} fusion(s32[2048]{0:T(1024)S(1)} %get-tuple-element.162, u32[2048]{0:T(1024)S(1)} %broadcast_clamp_fusion.5), kind=kCustom, calls=%fused_computation.clone.clone.1 | custom fusion | bytes 24576 | tf_op jit(solution)/shard_map/jit(searchsorted)/jit(_searchsorted_scan_impl)/vmap(jit(_searchsorted_scan_impl))/while/body/eval_jaxpr/gather | solution.py:96
  176.6 8.0 %scatter_custom_fusion = s32[2048]{0:T(1024)S(1)} fusion(s32[2048]{0:T(1024)S(1)} %get-tuple-element.112, s32[2048]{0:T(1024)S(1)} %convert_subtract_fusion, s32[]{:T(128)} %constant.77.clone.1), kind=kCustom, calls=%fused_computation.80 | custom fusion | bytes 8196 | tf_op jit(solution)/shard_map/scatter | solution.py:100
  184.7 1.2 fusion.40
  186.0 5.7 all-reduce.1
  191.7 1.2 add_convert_fusion
  192.9 21.3 %scatter_custom_fusion.1 = bf16[4032,512]{1,0:T(8,128)(2,1)} fusion(s32[2048]{0:T(1024)S(1)} %get-tuple-element.110, bf16[256,512]{1,0:T(8,128)(2,1)S(1)} %add_convert_fusion, s32[2048]{0:T(1024)S(1)} %get-tuple-element.115, bf16[]{:T(256)} %constant.75.clone.1), kind=kCustom, calls=%fused_computation.26 | custom fusion | bytes 4128770 | tf_op jit(solution)/shard_map/scatter | solution.py:105
  214.2 5.8 all-to-all-start
  220.0 11.7 %copy.38 = bf16[512,8064]{0,1:T(8,128)(2,1)} copy(bf16[512,8064]{1,0:T(8,128)(2,1)} %param.22) | data formatting | bytes 16515072 | tf_op args[8]
  231.7 77.5 %all-to-all-done = bf16[8,504,512]{2,1,0:T(8,128)(2,1)} async-done(((bf16[8,504,512]{2,1,0:T(8,128)(2,1)}), bf16[8,504,512]{2,1,0:T(8,128)(2,1)}, u32[]{:S(2)}, u32[]{:S(2)}) %all-to-all-start) | async-done | bytes 4128800 | tf_op jit(solution)/shard_map/all_to_all | solution.py:112
  309.2 8.9 %fusion.6 = f32[8,63,8,128]{3,2,0,1:T(8,128)} fusion(bf16[512,63,128,1]{0,2,3,1:T(8,128)(2,1)} %bitcast.74, bf16[8,504,512]{2,1,0:T(8,128)(2,1)} %all-to-all-done), kind=kOutput, calls=%fused_computation.33 | convolution fusion | flops 528482304 | bytes 14450688 | tf_op jit(solution)/shard_map/slmd,dlt->slmt/dot_general | solution.py:129
  318.2 0.7 copy-done.2
  318.8 13.1 %gather_fusion.5 = s32[2048]{0:T(1024)S(1)} fusion(s32[256]{0:T(256)S(1)} %copy-done.2, s32[2048]{0:T(1024)S(1)} %get-tuple-element.115), kind=kCustom, calls=%fused_computation.6 | custom fusion | bytes 24576 | tf_op jit(solution)/shard_map/gather | solution.py:110
  332.0 13.1 %gather_fusion.4 = s32[2048]{0:T(1024)S(1)} fusion(s32[256]{0:T(256)S(1)} %copy-done.1, s32[2048]{0:T(1024)S(1)} %get-tuple-element.115), kind=kCustom, calls=%fused_computation.5 | custom fusion | bytes 24576 | tf_op jit(solution)/shard_map/gather | solution.py:106
  345.1 8.1 %scatter_custom_fusion.2 = s32[4032]{0:T(1024)S(1)} fusion(s32[2048]{0:T(1024)S(1)} %get-tuple-element.110, s32[2048]{0:T(1024)S(1)} %fusion.33, s32[]{:T(128)} %constant.93.clone.1), kind=kCustom, calls=%fused_computation.72 | custom fusion | bytes 16132 | tf_op jit(solution)/shard_map/scatter | solution.py:110
  353.3 9.6 %all_to_all.58 = s32[8,1,504]{2,1,0:T(1,128)S(1)} all-to-all(s32[8,1,504]{2,1,0:T(1,128)S(1)} %all_to_all.41), channel_id=1, replica_groups=mesh['src'=4,'vocab'=8] {'vocab'}, dimensions={0} | all-to-all | bytes 32256 | tf_op jit(solution)/shard_map/all_to_all | solution.py:119
  363.0 0.2 eq.30
  363.3 7.6 %all-reduce.4.cloned.1.call-done = f32[8,63,8,128]{3,2,0,1:T(8,128)} async-done(((f32[8,63,8,128]{3,2,0,1:T(8,128)}), f32[8,63,8,128]{3,2,0,1:T(8,128)}) %all-reduce.4.cloned.1.call-update) | async-done | bytes 2064400 | tf_op jit(solution)/shard_map/psum | solution.py:132
  370.9 2.2 reduce_max.28
  373.1 4.1 select_reduce_fusion
  377.3 0.8 all_to_all.50
  378.0 5.5 all-to-all-start.4
  383.6 0.8 all_to_all.48
  384.3 2.5 all-to-all-done.4
  386.9 5.3 all-to-all-start.1
  392.2 0.8 all_to_all.49
  393.1 11.8 %gather_fusion.6 = f32[2048]{0:T(1024)S(1)} fusion(f32[4032]{0:T(1024)S(1)} %reshape.146, s32[2048]{0:T(1024)S(1)} %get-tuple-element.109), kind=kCustom, calls=%fused_computation.7 | custom fusion | bytes 24576 | tf_op jit(solution)/shard_map/gather | solution.py:159
  405.0 5.5 all-to-all-start.2
  410.5 0.2 select_reduce_fusion.1
  410.8 11.8 %gather_fusion.2 = f32[2048]{0:T(1024)S(1)} fusion(f32[4032]{0:T(1024)S(1)} %reshape.142, s32[2048]{0:T(1024)S(1)} %get-tuple-element.109), kind=kCustom, calls=%fused_computation.3 | custom fusion | bytes 24576 | tf_op jit(solution)/shard_map/gather | solution.py:157
  422.9 11.8 %gather_fusion.3 = f32[2048]{0:T(1024)S(1)} fusion(f32[4032]{0:T(1024)S(1)} %reshape.144, s32[2048]{0:T(1024)S(1)} %get-tuple-element.109), kind=kCustom, calls=%fused_computation.4 | custom fusion | bytes 24576 | tf_op jit(solution)/shard_map/gather | solution.py:158
  434.8 0.2 multiply_reduce_fusion.3
  435.0 0.6 fusion.41
  435.6 13.1 %gather_fusion.7 = f32[2048]{0:T(1024)S(1)} fusion(f32[256]{0:T(256)S(1)} %get-tuple-element.108, s32[2048]{0:T(1024)S(1)} %get-tuple-element.115), kind=kCustom, calls=%fused_computation.8 | custom fusion | bytes 24576 | tf_op jit(solution)/shard_map/gather | solution.py:167
  448.7 8.1 %scatter_custom_fusion.3 = f32[4032]{0:T(1024)S(1)} fusion(s32[2048]{0:T(1024)S(1)} %get-tuple-element.110, f32[2048]{0:T(1024)S(1)} %gather_fusion.7, f32[]{:T(128)} %constant.85.clone.1), kind=kCustom, calls=%fused_computation.67 | custom fusion | bytes 16132 | tf_op jit(solution)/shard_map/scatter | solution.py:167
  456.9 8.6 %all_to_all.59 = f32[8,1,504]{2,1,0:T(1,128)S(1)} all-to-all(f32[8,1,504]{2,1,0:T(1,128)S(1)} %all_to_all.45), channel_id=1, replica_groups=mesh['src'=4,'vocab'=8] {'vocab'}, dimensions={0} | all-to-all | bytes 32256 | tf_op jit(solution)/shard_map/all_to_all | solution.py:168
  465.9 6.4 %convert_bitcast_fusion = bf16[8,63,8,512]{3,2,0,1:T(8,128)(2,1)S(1)} fusion(bf16[512,63,128,1]{0,2,3,1:T(8,128)(2,1)} %bitcast.75, f32[8,63,8,128]{3,2,0,1:T(8,128)} %all-reduce.4.cloned.1.call-done, f32[8,63,8]{2,0,1:T(8,128)S(1)} %copy.48, s32[8,63,8]{2,0,1:T(8,128)S(1)} %copy.45), kind=kOutput, calls=%fused_computation.24 | convolution fusion | flops 533127168 | bytes 14482944 | tf_op jit(solution)/shard_map/slmt,dlt->slmd/dot_general | solution.py:177
  472.3 0.3 copy.79
  472.6 92.5 %all_to_all.60 = bf16[8,504,512]{2,1,0:T(8,128)(2,1)S(1)} all-to-all(bf16[8,504,512]{2,1,0:T(8,128)(2,1)S(1)} %bitcast.77), channel_id=1, replica_groups=mesh['src'=4,'vocab'=8] {'vocab'}, dimensions={0} | all-to-all | bytes 8257536 | tf_op jit(solution)/shard_map/all_to_all | solution.py:180
  565.1 4.6 bitcast_convert_fusion
  569.7 12.9 %gather_fusion.8 = f32[2048,512]{1,0:T(8,128)} fusion(f32[4032,512]{1,0:T(8,128)} %bitcast_convert_fusion, s32[2048]{0:T(1024)S(1)} %get-tuple-element.109), kind=kCustom, calls=%fused_computation.9 | custom fusion | bytes 8396800 | tf_op jit(solution)/shard_map/gather | solution.py:188
  582.6 3.3 bitcast_reduce_fusion
  585.9 0.2 multiply_reduce_fusion.2
  586.1 8.3 %all-reduce = (f32[256]{0:T(256)S(1)}, f32[256]{0:T(256)S(1)}) all-reduce(f32[256]{0:T(256)S(1)} %get-tuple-element.92, f32[256]{0:T(256)S(1)} %get-tuple-element.91), channel_id=1, replica_groups=mesh['src'=4,'vocab'=8] {'src'}, use_global_device_ids=true, to_apply=%region_25.26 | all-reduce | flops 512 | bytes 4096 | tf_op jit(solution)/shard_map/psum | solution.py:190
  594.5 1.0 subtract_multiply_fusion
  (104 shorter events, 2.5 us)
Async XLA Ops:
  7.2 7.8 %copy-start = (bf16[512,2048]{1,0:T(8,128)(2,1)S(1)}, bf16[512,2048]{1,0:T(8,128)(2,1)}, u32[]{:S(2)}) copy-start(bf16[512,2048]{1,0:T(8,128)(2,1)} %param.18) | copy-start | bytes 6291460
  7.2 177.5 %reduce-scatter.2.cloned.1.call-start = ((), (), s32[]{:S(2)}) async-start(), calls=%async_computation.8 | async-start | bytes 2621440 | tf_op jit(solution)/shard_map/reduce_scatter | solution.py:70
  14.9 2.2 copy-start.6
  34.2 150.6 %copy-start.4 = (bf16[256,512]{1,0:T(8,128)(2,1)S(1)}, bf16[256,512]{1,0:T(8,128)(2,1)}, u32[]{:S(2)}) copy-start(bf16[256,512]{1,0:T(8,128)(2,1)} %param.19) | copy-start | bytes 786436
  34.2 157.5 %copy-start.5 = (f32[512]{0:T(512)S(1)}, f32[512]{0:T(512)}, u32[]{:S(2)}) copy-start(f32[512]{0:T(512)} %param.20) | copy-start | bytes 6148
  34.2 157.5 %copy-start.7 = (f32[512]{0:T(512)S(1)}, f32[512]{0:T(512)}, u32[]{:S(2)}) copy-start(f32[512]{0:T(512)} %param.21) | copy-start | bytes 6148
  214.2 95.1 %all-to-all-start = ((bf16[8,504,512]{2,1,0:T(8,128)(2,1)}), bf16[8,504,512]{2,1,0:T(8,128)(2,1)}, u32[]{:S(2)}, u32[]{:S(2)}) async-start(bf16[8,504,512]{2,1,0:T(8,128)(2,1)} %bitcast.76), calls=%async_computation.1 | async-start | bytes 8257536 | tf_op jit(solution)/shard_map/all_to_all | solution.py:112
  220.0 150.9 %all-reduce.4.cloned.1.call-start = ((), (), s32[]{:S(2)}) async-start(), calls=%async_computation.9 | async-start | bytes 4128768 | tf_op jit(solution)/shard_map/psum | solution.py:132
  318.2 0.7 copy-start.2
  318.8 13.1 %copy-start.1 = (s32[256]{0:T(256)S(1)}, s32[256]{0:T(256)}, u32[]{:S(2)}) copy-start(s32[256]{0:T(256)} %param.24) | copy-start | bytes 3076
  378.0 8.9 %all-to-all-start.4 = ((f32[8,1,504]{2,1,0:T(1,128)}), f32[8,1,504]{2,1,0:T(1,128)S(1)}, u32[]{:S(2)}, u32[]{:S(2)}) async-start(f32[8,1,504]{2,1,0:T(1,128)} %all_to_all.50), calls=%async_computation.5 | async-start | bytes 32768 | tf_op jit(solution)/shard_map/all_to_all | solution.py:149
  386.9 18.1 %all-to-all-start.1 = ((f32[8,1,504]{2,1,0:T(1,128)}), f32[8,1,504]{2,1,0:T(1,128)S(1)}, u32[]{:S(2)}, u32[]{:S(2)}) async-start(f32[8,1,504]{2,1,0:T(1,128)} %all_to_all.48), calls=%async_computation.2 | async-start | bytes 32768 | tf_op jit(solution)/shard_map/all_to_all | solution.py:135
  405.0 17.8 %all-to-all-start.2 = ((f32[8,1,504]{2,1,0:T(1,128)}), f32[8,1,504]{2,1,0:T(1,128)S(1)}, u32[]{:S(2)}, u32[]{:S(2)}) async-start(f32[8,1,504]{2,1,0:T(1,128)} %all_to_all.49), calls=%async_computation.3 | async-start | bytes 32768 | tf_op jit(solution)/shard_map/all_to_all | solution.py:142
  582.6 3.3 copy-start.3
Sparse Core Ops, SparseCore 0:
  17.2 32.5 reduce-scatter.1
  318.3 52.5 all-reduce.3
where the time goes:
time: 607 us; the launch traced here: 602 us
  local copies, waits for them, and re-layouts  306 us (50%)
  blocking collectives  125 us (21%)
  waiting for transfers between devices  87.7 us (14%)
  other arithmetic  24.6 us (4%)
  starting transfers between devices  22.1 us (4%)
  matrix products  21.5 us (4%)
  between operations  15.3 us (3%)
    gather x12, local copies, waits for them, and re-layouts, shards(): firsts = jnp.searchsorted(sorted_ids, sorted_ids, side='left')  141 us
    all_to_all x1, blocking collectives, shards(): lax.all_to_all(grad_slots.reshape(voc_count, blocks_dev * bucket_most, wi...  92.5 us
    all_to_all x1, waiting for transfers between devices, shards(): lax.all_to_all(outgoing.reshape(voc_count, blocks_dev * bucket_most, widt...  77.5 us
    scatter x1, local copies, waits for them, and re-layouts, shards(): jnp.zeros((slot_total, width_dev), jnp.bfloat16).at[slot_ids]  21.3 us
    gather x1, local copies, waits for them, and re-layouts, shards(): is_target = pair_lists == target_slot[pair_rows]  13.1 us
    gather x1, local copies, waits for them, and re-layouts, shards(): target_offset[pair_rows]  13.1 us
    gather x1, local copies, waits for them, and re-layouts, shards(): log_total[pair_rows]  13.1 us
    gather x1, local copies, waits for them, and re-layouts, shards(): returned[slot_ids].reshape(row_count, list_count, width_dev)  12.9 us
  transfers between devices with their start and end apart: 6, of which 3 were waited for; matrix products, arithmetic and copies ran while one was open for 39% of the time, Pallas kernels for 0%

commit v1 on v0

v1 whole, which is shorter than its diff:
```python
import math

import jax
import jax.numpy as jnp
from jax import lax
from jax.sharding import PartitionSpec as P

HD = 128
BLK = 128


MASKED = -1e30
EPSILON = 1e-05


def shards(
    queries,
    enc_keys,
    enc_values,
    source_lengths,
    out_proj,
    dec_state,
    norm_gain,
    norm_bias,
    head_weight,
    shortlist,
    target_slot,
    target_offset,
):
    voc_count = lax.axis_size("vocab")
    row_count = queries.shape[0]
    mem_count = enc_keys.shape[1]
    model_width = out_proj.shape[1]
    width_dev = dec_state.shape[1]
    heads_dev = enc_keys.shape[2] // HD
    facts = lax.all_gather(
        jnp.concatenate([shortlist.T, target_slot[None], target_offset[None]], axis=0),
        "vocab",
        axis=0,
    )
    q_heads = queries.reshape(row_count, heads_dev, HD)
    key_heads = enc_keys[0].reshape(mem_count, heads_dev, HD)
    value_heads = enc_values[0].reshape(mem_count, heads_dev, HD)
    scores = jnp.einsum("rhe,phe->hrp", q_heads, key_heads, preferred_element_type=jnp.float32) * (
        1.0 / math.sqrt(HD)
    )
    positions = lax.iota(jnp.int32, mem_count)
    usable = (positions < source_lengths[0])[None, None, :]
    scores = jnp.where(usable, scores, MASKED)
    row_top = jnp.max(scores, axis=-1)
    raw_weights = jnp.where(usable, jnp.exp(scores - row_top[..., None]), 0.0)
    totals = jnp.sum(raw_weights, axis=-1)
    mixture = jnp.einsum(
        "hrp,phe->rhe",
        raw_weights.astype(jnp.bfloat16),
        value_heads,
        preferred_element_type=jnp.float32,
    )
    own_mix = mixture / totals.T[..., None]
    attn_own = own_mix.astype(jnp.bfloat16).reshape(row_count, heads_dev * HD)
    projected = lax.psum_scatter(
        lax.dot_general(
            out_proj, attn_own, (((0,), (1,)), ((), ())), preferred_element_type=jnp.float32
        ),
        "src",
        scatter_dimension=0,
        tiled=True,
    )
    residual = dec_state.astype(jnp.float32) + projected.T
    sum_rows, square_rows = lax.psum(
        (jnp.sum(residual, axis=1), jnp.sum(residual * residual, axis=1)), "src"
    )
    row_mean = sum_rows / model_width
    variance = square_rows / model_width - row_mean * row_mean
    inv_std = lax.rsqrt(variance + EPSILON)
    centered = (residual - row_mean[:, None]) * inv_std[:, None]
    normed = (centered * norm_gain + norm_bias).astype(jnp.bfloat16)
    list_count = shortlist.shape[1]
    blocks_dev = head_weight.shape[1] // BLK
    vocab_blocks = blocks_dev * voc_count
    bucket_most = max(2, 2 * row_count * list_count // vocab_blocks)
    voc_own = lax.axis_index("vocab")
    local_ids = facts[:, :list_count] - voc_own * blocks_dev
    block_iota = lax.broadcasted_iota(jnp.int32, (1, blocks_dev, 1), 1)
    lists = jnp.zeros((voc_count, blocks_dev, row_count), jnp.bool_)
    codes = jnp.full((voc_count, blocks_dev, row_count), -1, jnp.int32)
    for k in range(list_count):
        named = local_ids[:, k][:, None, :] == block_iota
        lists = lists | named
        aimed = named & (facts[:, list_count] == k)[:, None, :]
        codes = jnp.where(aimed, facts[:, list_count + 1][:, None, :], codes)
    earlier = (
        lax.broadcasted_iota(jnp.int32, (row_count, row_count), 0)
        < lax.broadcasted_iota(jnp.int32, (row_count, row_count), 1)
    ).astype(jnp.bfloat16)
    ranks = jnp.einsum(
        "slr,rq->slq", lists.astype(jnp.bfloat16), earlier, preferred_element_type=jnp.float32
    ).astype(jnp.int32)
    rank_iota = lax.broadcasted_iota(jnp.int32, (1, 1, bucket_most, 1), 2)
    holds = lists[:, :, None, :] & (ranks[:, :, None, :] == rank_iota)
    places = holds.astype(jnp.bfloat16)
    slot_codes = jnp.max(jnp.where(holds, codes[:, :, None, :], -1), axis=3)
    normed_all = lax.all_gather(normed, "vocab", axis=0)
    received = jnp.einsum(
        "slmr,srd->slmd", places, normed_all, preferred_element_type=jnp.float32
    ).astype(jnp.bfloat16)
    weight_view = head_weight.reshape(width_dev, blocks_dev, BLK)
    partial_logits = jnp.einsum(
        "slmd,dlt->slmt", received, weight_view, preferred_element_type=jnp.float32
    )
    full_logits = lax.psum(partial_logits, "src")
    slot_top = jnp.max(full_logits, axis=3)
    row_high = jnp.max(jnp.where(holds, slot_top[..., None], MASKED), axis=(1, 2))
    slot_high = jnp.sum(jnp.where(holds, row_high[:, None, None, :], 0.0), axis=3)
    slot_spread = jnp.sum(jnp.exp(full_logits - slot_high[..., None]), axis=3)
    offsets = lax.broadcasted_iota(jnp.int32, full_logits.shape, 3)
    target_hit = offsets == slot_codes[..., None]
    slot_pick = jnp.sum(jnp.where(target_hit, full_logits, 0.0), axis=3)
    row_spread = jnp.sum(jnp.where(holds, slot_spread[..., None], 0.0), axis=(1, 2))
    row_pick = jnp.sum(jnp.where(holds, slot_pick[..., None], 0.0), axis=(1, 2))
    stats = lax.all_gather(jnp.stack([row_high, row_spread, row_pick]), "vocab", axis=0)
    best = jnp.max(stats[:, 0], axis=0)
    log_total = best + jnp.log(jnp.sum(jnp.exp(stats[:, 0] - best) * stats[:, 1], axis=0))
    row_loss = lax.dynamic_index_in_dim(
        log_total - jnp.sum(stats[:, 2], axis=0), voc_own, axis=0, keepdims=False
    )
    slot_total = jnp.sum(jnp.where(holds, log_total[:, None, None, :], 0.0), axis=3)
    deltas = (
        jnp.exp(full_logits - slot_total[..., None]) - target_hit.astype(jnp.float32)
    ).astype(jnp.bfloat16)
    grad_slots = jnp.einsum(
        "slmt,dlt->slmd", deltas, weight_view, preferred_element_type=jnp.float32
    ).astype(jnp.bfloat16)
    grad_rows = jnp.einsum(
        "slmr,slmd->srd", places, grad_slots, preferred_element_type=jnp.float32
    ).astype(jnp.bfloat16)
    returned = lax.all_to_all(grad_rows, "vocab", split_axis=0, concat_axis=0, tiled=True)
    grad_normed = jnp.sum(returned.astype(jnp.float32), axis=0)
    gained = grad_normed * norm_gain
    sum_g, sum_gx = lax.psum((jnp.sum(gained, axis=1), jnp.sum(gained * centered, axis=1)), "src")
    grad_state = inv_std[:, None] * (
        gained - (sum_g / model_width)[:, None] - centered * (sum_gx / model_width)[:, None]
    )
    return (row_loss, grad_state)


def solution(mesh):
    placed = (
        P("vocab", "src"),
        P("vocab", None, "src"),
        P("vocab", None, "src"),
        P("vocab"),
        P("src", None),
        P("vocab", "src"),
        P("src"),
        P("src"),
        P("src", "vocab"),
        P("vocab", None),
        P("vocab"),
        P("vocab"),
    )
    return jax.shard_map(
        shards,
        mesh=mesh,
        in_specs=placed,
        out_specs=(P("vocab"), P("vocab", "src")),
        check_vma=False,
    )
```

time: 607 us -> 296 us (0.49)
  local copies, waits for them, and re-layouts: 306 us -> 18.8 us
  blocking collectives: 125 us -> 58.5 us
  waiting for transfers between devices: 87.7 us -> 135 us
  starting transfers between devices: 22.1 us -> 8.39 us
  matrix products: 21.5 us -> 30.3 us
    gather x20 -> x0, local copies, waits for them, and re-layouts: 241 us -> none  [the longest x12 141 us: shards(): firsts = jnp.searchsorted(sorted_ids, sorted_ids, side='left')]
    all_to_all x3 -> x0, blocking collectives: 111 us -> none  [the longest x1 92.5 us: shards(): lax.all_to_all(grad_slots.reshape(voc_count, blocks_dev * bucket_most, wi...]
    scatter x4 -> x0, local copies, waits for them, and re-layouts: 45.4 us -> none  [the longest x1 21.3 us: shards(): jnp.zeros((slot_total, width_dev), jnp.bfloat16).at[slot_ids]]
    all_gather x0 -> x2, blocking collectives: none -> 45.2 us  [the longest x1 23.2 us: shards(): lax.all_gather(jnp.concatenate([shortlist.T, target_slot[None], target_of...]
    psum x1, waiting for transfers between devices: 7.6 us -> 48.6 us  [shards(): full_logits = lax.psum(partial_logits, 'src')]
    all_to_all x4 -> x1, waiting for transfers between devices: 80 us -> 42.3 us  [shards(): lax.all_to_all(grad_rows, 'vocab', split_axis=0, concat_axis=0, tiled=True)]
    reduce_scatter x1, waiting for transfers between devices: 0.02 us -> 32.6 us  [shards(): lax.psum_scatter(lax.dot_general(out_proj, attn_own, (((0,), (1,)), ((),...]
    all_to_all x4 -> x1, starting transfers between devices: 22 us -> 8.26 us  [shards(): lax.all_to_all(grad_rows, 'vocab', split_axis=0, concat_axis=0, tiled=True)]
  transfers between devices with their start and end apart: 6 -> 4, of which waited for: 3 -> 4; matrix products, arithmetic and copies ran while one was open for 39% -> 6% of each run, Pallas kernels for 0% -> 0%
where the time goes in v1:
time: 296 us; the launch traced here: 290 us
  waiting for transfers between devices  135 us (46%)
  blocking collectives  58.5 us (20%)
  matrix products  30.3 us (10%)
  other arithmetic  24.2 us (8%)
  local copies, waits for them, and re-layouts  18.8 us (6%)
  between operations  14.8 us (5%)
  starting transfers between devices  8.39 us (3%)
    psum x1, waiting for transfers between devices, shards(): full_logits = lax.psum(partial_logits, 'src')  48.6 us
    all_to_all x1, waiting for transfers between devices, shards(): lax.all_to_all(grad_rows, 'vocab', split_axis=0, concat_axis=0, tiled=True)  42.3 us
    reduce_scatter x1, waiting for transfers between devices, shards(): lax.psum_scatter(lax.dot_general(out_proj, attn_own, (((0,), (1,)), ((),...  32.6 us
    all_gather x1, blocking collectives, shards(): lax.all_gather(jnp.concatenate([shortlist.T, target_slot[None], target_of...  23.2 us
    all_gather x1, blocking collectives, shards(): lax.all_gather(jnp.stack([row_high, row_spread, row_pick]), 'vocab', axis=0)  22 us
    unnamed x26, local copies, waits for them, and re-layouts  12.5 us
    all_gather x1, waiting for transfers between devices, shards(): normed_all = lax.all_gather(normed, 'vocab', axis=0)  11.8 us
    dot_general x1, matrix products, shards(): jnp.einsum('slmd,dlt->slmt', received, weight_view, preferred_element_typ...  8.99 us
  transfers between devices with their start and end apart: 4, of which 4 were waited for; matrix products, arithmetic and copies ran while one was open for 6% of the time, Pallas kernels for 0%

profile of v1, /device:TPU:11, one launch (start us, length us, event | category | flops | bytes accessed | tf_op | source)
XLA Modules:
  0.0 290.4 jit_solution(15207635742679180929)
XLA Ops:
  7.2 0.0 copy-start
  7.2 0.0 copy-start.4
  7.2 0.0 reduce-scatter.2.cloned.1.call-start
  8.1 1.0 reshape_squeeze.6
  9.1 1.5 fusion.64
  10.6 2.2 fusion.22
  12.8 0.0 copy-done.4
  12.8 0.1 copy.48
  12.9 0.0 copy-start.2
  13.0 2.0 fusion.24
  14.9 0.0 copy-start.5
  15.0 0.0 copy-start.7
  15.0 0.0 copy-done
  15.0 2.1 convolution_bitcast_fusion
  17.1 0.0 reduce-scatter.2.cloned.1.call-update
  17.1 0.0 all-gather.6.cloned.1.call-start
  17.1 32.6 %reduce-scatter.2.cloned.1.call-done = f32[512,256]{0,1:T(8,128)} async-done(((f32[2048,256]{0,1:T(8,128)}), f32[512,256]{0,1:T(8,128)}) %reduce-scatter.2.cloned.1.call-update) | async-done | bytes 524304 | tf_op jit(solution)/shard_map/reduce_scatter | solution.py:61
  49.8 0.0 copy-done.2
  49.8 1.2 fusion.59
  51.0 5.7 %all-reduce.1 = (f32[256]{0:T(256)S(1)}, f32[256]{0:T(256)S(1)}) all-reduce(f32[256]{0:T(256)S(1)} %get-tuple-element.5, f32[256]{0:T(256)S(1)} %get-tuple-element.4), channel_id=1, replica_groups=mesh['src'=4,'vocab'=8] {'src'}, use_global_device_ids=true, to_apply=%region_6.7 | all-reduce | flops 512 | bytes 4096 | tf_op jit(solution)/shard_map/psum | solution.py:70
  56.7 0.0 copy-done.5
  56.8 0.0 copy-done.7
  56.8 1.9 add_convert_fusion
  58.7 0.0 all-gather.6.cloned.1.call-update
  58.7 0.0 all-reduce.4.cloned.1.call-start
  58.8 0.0 copy-start.6
  58.8 0.0 copy-start.8
  58.8 0.0 copy-start.9
  58.8 11.8 %copy.32 = bf16[512,8064]{0,1:T(8,128)(2,1)} copy(bf16[512,8064]{1,0:T(8,128)(2,1)} %param.20) | data formatting | bytes 16515072 | tf_op args[8]
  70.6 0.0 copy-done.6
  70.6 23.2 %all-gather.3 = s32[8,10,256]{2,1,0:T(8,128)S(1)} all-gather(s32[1,10,256]{2,1,0:T(8,128)S(1)} %add_bitcast_fusion), channel_id=2, replica_groups=mesh['src'=4,'vocab'=8] {'vocab'}, dimensions={0}, use_global_device_ids=true | all-gather | bytes 92160 | tf_op jit(solution)/shard_map/all_gather | solution.py:36
  93.9 0.5 fusion.29
  94.4 0.6 convolution_convert_fusion
  95.0 1.7 fusion.3
  96.8 11.8 %all-gather.6.cloned.1.call-done = bf16[2048,512]{1,0:T(8,128)(2,1)} async-done(((bf16[256,512]{1,0:T(8,128)(2,1)}), bf16[2048,512]{1,0:T(8,128)(2,1)}) %all-gather.6.cloned.1.call-update) | async-done | bytes 2097168 | tf_op jit(solution)/shard_map/all_gather | solution.py:103
  108.6 9.0 %fusion.14 = f32[8,63,8,128]{3,2,0,1:T(8,128)} fusion(bf16[512,63,128,1]{0,2,3,1:T(8,128)(2,1)} %bitcast.126, bf16[8,256,512,1]{2,1,0,3:T(8,128)(2,1)} %bitcast.141, pred[8,63,8,256]{3,1,2,0:T(8,128)(4,1)} %fusion.3), kind=kOutput, calls=%fused_computation.23 | convolution fusion | flops 1587511296 | bytes 13451264 | tf_op jit(solution)/shard_map/slmd,dlt->slmt/dot_general | solution.py:108
  117.6 0.0 all-reduce.4.cloned.1.call-update
  117.7 1.1 select_select_fusion
  118.8 1.3 select_reduce_fusion.2
  120.0 0.2 copy.38
  120.2 48.6 %all-reduce.4.cloned.1.call-done = f32[8,63,8,128]{3,2,0,1:T(8,128)} async-done(((f32[8,63,8,128]{3,2,0,1:T(8,128)}), f32[8,63,8,128]{3,2,0,1:T(8,128)}) %all-reduce.4.cloned.1.call-update) | async-done | bytes 2064400 | tf_op jit(solution)/shard_map/psum | solution.py:111
  168.8 2.9 reduce_max.46
  171.7 1.1 copy.34
  172.8 1.0 select_reduce_fusion.5
  173.8 0.9 select_reduce_fusion.4
  174.7 0.9 copy.35
  175.5 4.7 %exponential_reduce_fusion = (f32[8,63,8]{2,0,1:T(8,128)}, f32[8,63,8]{2,0,1:T(8,128)}) fusion(f32[8,63,8,128]{3,2,0,1:T(8,128)} %all-reduce.4.cloned.1.call-done, f32[8,63,8]{2,0,1:T(8,128)} %copy.35, s32[8,63,8]{2,0,1:T(8,128)S(1)} %copy.38), kind=kLoop, calls=%fused_computation.22 | loop fusion | flops 2572416 | bytes 2128896 | tf_op jit(solution)/shard_map/reduce_sum | solution.py:115
  180.2 1.1 copy.36
  181.3 1.1 copy.39
  182.4 1.3 select_reduce_fusion.3
  183.7 22.0 %all-gather.2 = f32[24,8,256]{2,1,0:T(8,128)S(1)} all-gather(f32[3,8,256]{2,1,0:T(8,128)S(1)} %pad_maximum_fusion), channel_id=4, replica_groups=mesh['src'=4,'vocab'=8] {'vocab'}, dimensions={0}, use_global_device_ids=true | all-gather | bytes 221184 | tf_op jit(solution)/shard_map/all_gather | solution.py:121
  205.8 0.7 copy-done.3
  206.5 0.9 select_reduce_fusion
  207.4 0.9 copy.41
  208.2 6.4 %convert_bitcast_fusion = bf16[8,63,8,512]{3,2,0,1:T(8,128)(2,1)S(1)} fusion(bf16[512,63,128,1]{0,2,3,1:T(8,128)(2,1)} %bitcast.127, f32[8,63,8,128]{3,2,0,1:T(8,128)} %all-reduce.4.cloned.1.call-done, f32[8,63,8]{2,0,1:T(8,128)} %copy.41, s32[8,63,8]{2,0,1:T(8,128)S(1)} %copy.38), kind=kOutput, calls=%fused_computation.13 | convolution fusion | flops 533127168 | bytes 14482944 | tf_op jit(solution)/shard_map/slmt,dlt->slmd/dot_general | solution.py:131
  214.6 6.5 %bitcast_convert_fusion = bf16[8,256,512]{2,1,0:T(8,128)(2,1)} fusion(bf16[8,63,8,512]{3,2,0,1:T(8,128)(2,1)S(1)} %convert_bitcast_fusion, s32[8,63,256]{2,1,0:T(8,128)S(1)} %convolution_convert_fusion, pred[8,63,256]{2,1,0:T(8,128)(4,1)S(1)} %fusion.29), kind=kOutput, calls=%fused_computation.1 | convolution fusion | flops 1060077568 | bytes 6871040 | tf_op jit(solution)/shard_map/slmr,slmd->srd/dot_general | solution.py:134
  221.1 8.3 %all-to-all-start = ((bf16[8,256,512]{2,1,0:T(8,128)(2,1)}), bf16[8,256,512]{2,1,0:T(8,128)(2,1)}, u32[]{:S(2)}, u32[]{:S(2)}) async-start(bf16[8,256,512]{2,1,0:T(8,128)(2,1)} %bitcast_convert_fusion), calls=%async_computation.1 | async-start | bytes 4194304 | tf_op jit(solution)/shard_map/all_to_all | solution.py:137
  229.4 0.9 slice_reduce_fusion
  230.3 0.6 dynamic-slice_subtract_fusion
  230.8 42.3 %all-to-all-done = bf16[8,256,512]{2,1,0:T(8,128)(2,1)} async-done(((bf16[8,256,512]{2,1,0:T(8,128)(2,1)}), bf16[8,256,512]{2,1,0:T(8,128)(2,1)}, u32[]{:S(2)}, u32[]{:S(2)}) %all-to-all-start) | async-done | bytes 2097184 | tf_op jit(solution)/shard_map/all_to_all | solution.py:137
  273.1 1.9 convert_reduce_fusion
  275.0 0.2 multiply_reduce_fusion.2
  275.3 7.5 %all-reduce = (f32[256]{0:T(256)S(1)}, f32[256]{0:T(256)S(1)}) all-reduce(f32[256]{0:T(256)S(1)} %get-tuple-element.9, f32[256]{0:T(256)S(1)} %get-tuple-element.8), channel_id=1, replica_groups=mesh['src'=4,'vocab'=8] {'src'}, use_global_device_ids=true, to_apply=%region_24.25 | all-reduce | flops 512 | bytes 4096 | tf_op jit(solution)/shard_map/psum | solution.py:140
  282.8 1.0 subtract_multiply_fusion
  (23 shorter events, 0.2 us)
Async XLA Ops:
  7.2 7.8 %copy-start = (bf16[512,2048]{1,0:T(8,128)(2,1)S(1)}, bf16[512,2048]{1,0:T(8,128)(2,1)}, u32[]{:S(2)}) copy-start(bf16[512,2048]{1,0:T(8,128)(2,1)} %param.16) | copy-start | bytes 6291460
  7.2 5.6 %copy-start.4 = (bf16[1,256,512]{2,1,0:T(8,128)(2,1)S(1)}, bf16[1,256,512]{2,1,0:T(8,128)(2,1)}, u32[]{:S(2)}) copy-start(bf16[1,256,512]{2,1,0:T(8,128)(2,1)} %param.14) | copy-start | bytes 786436
  7.2 42.6 %reduce-scatter.2.cloned.1.call-start = ((), (), s32[]{:S(2)}) async-start(), calls=%async_computation.2 | async-start | bytes 2621440 | tf_op jit(solution)/shard_map/reduce_scatter | solution.py:61
  12.9 36.8 %copy-start.2 = (bf16[256,512]{1,0:T(8,128)(2,1)S(1)}, bf16[256,512]{1,0:T(8,128)(2,1)}, u32[]{:S(2)}) copy-start(bf16[256,512]{1,0:T(8,128)(2,1)} %param.17) | copy-start | bytes 786436
  14.9 41.8 %copy-start.5 = (f32[512]{0:T(512)S(1)}, f32[512]{0:T(512)}, u32[]{:S(2)}) copy-start(f32[512]{0:T(512)} %param.18) | copy-start | bytes 6148
  15.0 41.8 %copy-start.7 = (f32[512]{0:T(512)S(1)}, f32[512]{0:T(512)}, u32[]{:S(2)}) copy-start(f32[512]{0:T(512)} %param.19) | copy-start | bytes 6148
  17.1 91.5 %all-gather.6.cloned.1.call-start = ((), (), s32[]{:S(2)}) async-start(), calls=%async_computation.4 | async-start | bytes 2359296 | tf_op jit(solution)/shard_map/all_gather | solution.py:103
  58.7 110.1 %all-reduce.4.cloned.1.call-start = ((), (), s32[]{:S(2)}) async-start(), calls=%async_computation.3 | async-start | bytes 4128768 | tf_op jit(solution)/shard_map/psum | solution.py:111
  58.8 11.8 %copy-start.6 = (s32[256,8]{0,1:T(8,128)S(1)}, s32[256,8]{0,1:T(8,128)}, u32[]{:S(2)}) copy-start(s32[256,8]{0,1:T(8,128)} %param.21) | copy-start | bytes 24580
  58.8 11.8 %copy-start.8 = (s32[256]{0:T(256)S(1)}, s32[256]{0:T(256)}, u32[]{:S(2)}) copy-start(s32[256]{0:T(256)} %param.23) | copy-start | bytes 3076
  58.8 11.8 %copy-start.9 = (s32[256]{0:T(256)S(1)}, s32[256]{0:T(256)}, u32[]{:S(2)}) copy-start(s32[256]{0:T(256)} %param.22) | copy-start | bytes 3076
  205.8 0.7 copy-start.3
  221.1 53.9 %copy-start.1 = (f32[512,256]{0,1:T(8,128)S(1)}, f32[512,256]{0,1:T(8,128)}, u32[]{:S(2)}) copy-start(f32[512,256]{0,1:T(8,128)} %reduce-scatter.2.cloned.1.call-done) | copy-start | bytes 1572868
  221.1 51.9 %all-to-all-start = ((bf16[8,256,512]{2,1,0:T(8,128)(2,1)}), bf16[8,256,512]{2,1,0:T(8,128)(2,1)}, u32[]{:S(2)}, u32[]{:S(2)}) async-start(bf16[8,256,512]{2,1,0:T(8,128)(2,1)} %bitcast_convert_fusion), calls=%async_computation.1 | async-start | bytes 4194304 | tf_op jit(solution)/shard_map/all_to_all | solution.py:137
Sparse Core Ops, SparseCore 0:
  17.2 32.5 reduce-scatter.1
  58.8 49.7 all-gather.5
  117.7 51.0 all-reduce.3

commit v2 on v1

--- a/solution.py
+++ b/solution.py
@@ -1,8 +1,11 @@
+import functools
 import math
 
 import jax
 import jax.numpy as jnp
 from jax import lax
+from jax.experimental import pallas as pl
+from jax.experimental.pallas import tpu as pltpu
 from jax.sharding import PartitionSpec as P
 
 HD = 128
@@ -11,6 +14,121 @@
 
 MASKED = -1e30
 EPSILON = 1e-05
+
+
+VMEM_BYTES = 40 * 1024 * 1024
+MESH_ID = pl.DeviceIdType.MESH
+
+
+def greet(axis, partners):
+    barrier = pltpu.get_barrier_semaphore()
+    for partner in partners:
+        pl.semaphore_signal(barrier, inc=1, device_id={axis: partner}, device_id_type=MESH_ID)
+    pl.semaphore_wait(barrier, len(partners))
+
+
+def remote(axis, src, dst, send_sem, recv_sem, partner):
+    return pltpu.make_async_remote_copy(
+        src_ref=src,
+        dst_ref=dst,
+        send_sem=send_sem,
+        recv_sem=recv_sem,
+        device_id={axis: partner},
+        device_id_type=MESH_ID,
+    )
+
+
+def gather_body(axis, count, own_ref, all_ref, send_sems, recv_sems):
+    me = lax.axis_index(axis)
+    partners = [lax.rem(me + step, count) for step in range(1, count)]
+    greet(axis, partners)
+    copies = []
+    for i, partner in enumerate(partners):
+        copy = remote(
+            axis, own_ref, all_ref.at[me], send_sems.at[i], recv_sems.at[i], partner
+        )
+        copy.start()
+        copies.append(copy)
+    all_ref[me] = own_ref[...]
+    for copy in copies:
+        copy.wait()
+
+
+def gather_small(own, axis, collective_id):
+    count = lax.axis_size(axis)
+    return pl.pallas_call(
+        functools.partial(gather_body, axis, count),
+        out_shape=jax.ShapeDtypeStruct((count,) + own.shape, own.dtype),
+        in_specs=[pl.BlockSpec(memory_space=pltpu.VMEM)],
+        out_specs=pl.BlockSpec(memory_space=pltpu.VMEM),
+        scratch_shapes=[
+            pltpu.SemaphoreType.DMA((count - 1,)),
+            pltpu.SemaphoreType.DMA((count - 1,)),
+        ],
+        compiler_params=pltpu.CompilerParams(
+            collective_id=collective_id, has_side_effects=True, vmem_limit_bytes=VMEM_BYTES
+        ),
+    )(own)
+
+
+def src_places(axis, rings):
+    me = lax.axis_index(axis)
+    core = lax.rem(me, 2)
+    ring = me // 2
+    mate = me + 1 - 2 * core
+    others = [lax.rem(ring + step, rings) for step in range(1, rings)]
+    greet(axis, [mate] + [other * 2 + core for other in others])
+    return core, ring, mate, others
+
+
+def scatter_body(axis, rings, x_ref, o_ref, first, summed, second, sems):
+    core, ring, mate, others = src_places(axis, rings)
+    targets = others + [ring]
+    pairs = []
+    for i, target in enumerate(targets):
+        copy = remote(
+            axis, x_ref.at[target * 2 + 1 - core], first.at[i], sems.at[0, i], sems.at[1, i], mate
+        )
+        copy.start()
+        pairs.append(copy)
+    crossings = []
+    for i, target in enumerate(others):
+        pairs[i].wait_recv()
+        summed[i] = x_ref[target * 2 + core] + first[i]
+        copy = remote(
+            axis, summed.at[i], second.at[i], sems.at[2, i], sems.at[3, i], target * 2 + core
+        )
+        copy.start()
+        crossings.append(copy)
+    pairs[-1].wait_recv()
+    o_ref[...] = x_ref[ring * 2 + core] + first[rings - 1]
+    for i, copy in enumerate(crossings):
+        copy.wait_recv()
+        o_ref[...] += second[i]
+    for copy in pairs + crossings:
+        copy.wait_send()
+
+
+def scatter_sum(chunks, axis, collective_id):
+    count = chunks.shape[0]
+    rings = count // 2
+    piece = chunks.shape[1:]
+    crossing = max(rings - 1, 1)
+    return pl.pallas_call(
+        functools.partial(scatter_body, axis, rings),
+        out_shape=jax.ShapeDtypeStruct(piece, chunks.dtype),
+        in_specs=[pl.BlockSpec(memory_space=pltpu.VMEM)],
+        out_specs=pl.BlockSpec(memory_space=pltpu.VMEM),
+        scratch_shapes=[
+            pltpu.VMEM((rings,) + piece, chunks.dtype),
+            pltpu.VMEM((crossing,) + piece, chunks.dtype),
+            pltpu.VMEM((crossing,) + piece, chunks.dtype),
+            pltpu.SemaphoreType.DMA((4, rings)),
+        ],
+        compiler_params=pltpu.CompilerParams(
+            collective_id=collective_id, has_side_effects=True, vmem_limit_bytes=VMEM_BYTES
+        ),
+    )(chunks)
 
 
 def shards(
@@ -33,10 +151,8 @@
     model_width = out_proj.shape[1]
     width_dev = dec_state.shape[1]
     heads_dev = enc_keys.shape[2] // HD
-    facts = lax.all_gather(
-        jnp.concatenate([shortlist.T, target_slot[None], target_offset[None]], axis=0),
-        "vocab",
-        axis=0,
+    facts = gather_small(
+        jnp.concatenate([shortlist.T, target_slot[None], target_offset[None]], axis=0), "vocab", 1
     )
     q_heads = queries.reshape(row_count, heads_dev, HD)
     key_heads = enc_keys[0].reshape(mem_count, heads_dev, HD)
@@ -58,13 +174,12 @@
     )
     own_mix = mixture / totals.T[..., None]
     attn_own = own_mix.astype(jnp.bfloat16).reshape(row_count, heads_dev * HD)
-    projected = lax.psum_scatter(
+    projected = scatter_sum(
         lax.dot_general(
             out_proj, attn_own, (((0,), (1,)), ((), ())), preferred_element_type=jnp.float32
-        ),
+        ).reshape(-1, width_dev, row_count),
         "src",
-        scatter_dimension=0,
-        tiled=True,
+        2,
     )
     residual = dec_state.astype(jnp.float32) + projected.T
     sum_rows, square_rows = lax.psum(
@@ -118,7 +233,7 @@
     slot_pick = jnp.sum(jnp.where(target_hit, full_logits, 0.0), axis=3)
     row_spread = jnp.sum(jnp.where(holds, slot_spread[..., None], 0.0), axis=(1, 2))
     row_pick = jnp.sum(jnp.where(holds, slot_pick[..., None], 0.0), axis=(1, 2))
-    stats = lax.all_gather(jnp.stack([row_high, row_spread, row_pick]), "vocab", axis=0)
+    stats = gather_small(jnp.stack([row_high, row_spread, row_pick]), "vocab", 3)
     best = jnp.max(stats[:, 0], axis=0)
     log_total = best + jnp.log(jnp.sum(jnp.exp(stats[:, 0] - best) * stats[:, 1], axis=0))
     row_loss = lax.dynamic_index_in_dim(

time: 296 us -> 273 us (0.922)
  blocking collectives: 58.5 us -> 11.1 us
  Pallas kernels: 0 us -> 31.4 us
  waiting for transfers between devices: 135 us -> 122 us
  local copies, waits for them, and re-layouts: 18.8 us -> 30.7 us
  starting transfers between devices: 8.39 us -> 4.7 us
    all_gather x2 -> x0, blocking collectives: 45.2 us -> none  [the longest x1 23.2 us: shards(): lax.all_gather(jnp.concatenate([shortlist.T, target_slot[None], target_of...]
    reduce_scatter x1 -> x0, waiting for transfers between devices: 32.6 us -> none  [shards(): lax.psum_scatter(lax.dot_general(out_proj, attn_own, (((0,), (1,)), ((),...]
    pallas_call x0 -> x3, Pallas kernels: none -> 31.4 us  [the longest x1 16.3 us: scatter_sum(): pl.pallas_call(functools.partial(scatter_body, axis, rings), out_shape=ja...]
    all_gather x1, waiting for transfers between devices: 11.8 us -> 28.3 us  [shards(): normed_all = lax.all_gather(normed, 'vocab', axis=0)]
    all_gather x0 -> x1, local copies, waits for them, and re-layouts: none -> 3.9 us  [shards(): normed_all = lax.all_gather(normed, 'vocab', axis=0)]
    all_to_all x1, starting transfers between devices: 8.26 us -> 4.44 us  [shards(): lax.all_to_all(grad_rows, 'vocab', split_axis=0, concat_axis=0, tiled=True)]
    unnamed x26 -> x34, local copies, waits for them, and re-layouts: 12.5 us -> 15.6 us
  transfers between devices with their start and end apart: 4 -> 3, of which waited for: 4 -> 3; matrix products, arithmetic and copies ran while one was open for 6% -> 7% of each run, Pallas kernels for 0% -> 2%
where the time goes in v2:
time: 273 us; the launch traced here: 268 us
  waiting for transfers between devices  122 us (45%)
  Pallas kernels  31.4 us (12%)
  local copies, waits for them, and re-layouts  30.7 us (11%)
  matrix products  30.4 us (11%)
  other arithmetic  22.1 us (8%)
  between operations  15.2 us (6%)
  blocking collectives  11.1 us (4%)
  starting transfers between devices  4.7 us (2%)
    psum x1, waiting for transfers between devices, shards(): full_logits = lax.psum(partial_logits, 'src')  48.7 us
    all_to_all x1, waiting for transfers between devices, shards(): lax.all_to_all(grad_rows, 'vocab', split_axis=0, concat_axis=0, tiled=True)  44.9 us
    all_gather x1, waiting for transfers between devices, shards(): normed_all = lax.all_gather(normed, 'vocab', axis=0)  28.3 us
    pallas_call x1, Pallas kernels, scatter_sum(): pl.pallas_call(functools.partial(scatter_body, axis, rings), out_shape=ja...  16.3 us
    unnamed x34, local copies, waits for them, and re-layouts  15.6 us
    pallas_call x2, Pallas kernels, gather_small(): pl.pallas_call(functools.partial(gather_body, axis, count), out_shape=jax...  15.2 us
    dot_general x1, matrix products, shards(): jnp.einsum('slmd,dlt->slmt', received, weight_view, preferred_element_typ...  9.07 us
    dot_general x1, matrix products, shards(): jnp.einsum('slmr,slmd->srd', places, grad_slots, preferred_element_type=j...  6.5 us
  transfers between devices with their start and end apart: 3, of which 3 were waited for; matrix products, arithmetic and copies ran while one was open for 7% of the time, Pallas kernels for 2%

profile of v2, /device:TPU:11, one launch (start us, length us, event | category | flops | bytes accessed | tf_op | source)
XLA Modules:
  0.0 267.5 jit_solution(14416895154872669782)
XLA Ops:
  7.2 0.0 copy-start
  7.2 0.0 copy-start.4
  7.2 0.0 copy-start.5
  7.2 0.0 all-gather.3.cloned.1.call-start
  8.1 1.0 reshape_squeeze.6
  9.1 1.5 fusion.63
  10.5 2.2 fusion.22
  12.8 0.0 copy-done.4
  12.8 0.1 copy.33
  12.9 0.0 copy-done.5
  12.9 0.0 copy-start.2
  12.9 0.1 copy.58
  13.1 1.9 fusion.24
  15.0 0.0 copy-done
  15.0 2.1 convolution_bitcast_fusion
  17.1 0.0 copy-start.10
  17.1 2.9 %copy.38 = f32[2048,256]{1,0:T(8,128)} copy(f32[2048,256]{0,1:T(8,128)} %convolution_bitcast_fusion) | data formatting | bytes 4194304 | tf_op jit(solution)/shard_map/dot_general | solution.py:178
  20.1 1.6 copy-done.1
  21.7 16.3 %shard_map.132 = f32[512,256]{1,0:T(8,128)S(1)} custom-call(f32[4,512,256]{2,1,0:T(8,128)S(1)} %bitcast.122), custom_call_target="tpu_custom_call" | custom-call | tf_op jit(solution)/shard_map/pallas_call | solution.py:117
  38.0 0.1 fusion.59
  38.1 5.6 %all-reduce.1 = (f32[256]{0:T(256)S(1)}, f32[256]{0:T(256)S(1)}) all-reduce(f32[256]{0:T(256)S(1)} %get-tuple-element.11, f32[256]{0:T(256)S(1)} %get-tuple-element.10), channel_id=1, replica_groups=mesh['src'=4,'vocab'=8] {'src'}, use_global_device_ids=true, to_apply=%region_5.6 | all-reduce | flops 512 | bytes 4096 | tf_op jit(solution)/shard_map/psum | solution.py:185
  43.7 0.0 copy-done.2
  43.7 0.0 copy-done.6
  43.7 0.0 copy-done.8
  43.7 0.9 add_convert_fusion
  44.6 0.0 all-gather.3.cloned.1.call-update
  44.7 0.2 all-reduce.4.cloned.1.call-start
  44.9 6.3 %shard_map.131 = s32[8,10,256]{2,1,0:T(8,128)S(1)} custom-call(s32[10,256]{1,0:T(8,128)S(1)} %pad_add_fusion.own_ref), custom_call_target="tpu_custom_call" | custom-call | tf_op jit(solution)/shard_map/pallas_call | solution.py:59
  51.3 11.8 %copy.41 = bf16[512,8064]{0,1:T(8,128)(2,1)} copy(bf16[512,8064]{1,0:T(8,128)(2,1)} %param.20) | data formatting | bytes 16515072 | tf_op args[8]
  63.1 0.1 broadcast_compare_fusion.7
  63.3 0.5 fusion.29
  63.8 0.6 convolution_convert_fusion
  64.4 1.7 fusion.3
  66.1 28.3 %all-gather.3.cloned.1.call-done = bf16[2048,512]{0,1:T(8,128)(2,1)} async-done(((bf16[256,512]{0,1:T(8,128)(2,1)}), bf16[2048,512]{0,1:T(8,128)(2,1)}) %all-gather.3.cloned.1.call-update) | async-done | bytes 2097168 | tf_op jit(solution)/shard_map/all_gather | solution.py:218
  94.4 3.9 %copy.59 = bf16[2048,512]{1,0:T(8,128)(2,1)} copy(bf16[2048,512]{0,1:T(8,128)(2,1)} %all-gather.3.cloned.1.call-done) | data formatting | bytes 4194304 | tf_op jit(solution)/shard_map/all_gather | solution.py:218
  98.3 9.1 %fusion.14 = f32[8,63,8,128]{3,2,0,1:T(8,128)} fusion(bf16[512,63,128,1]{0,2,3,1:T(8,128)(2,1)} %bitcast.123, bf16[8,256,512,1]{2,1,0,3:T(8,128)(2,1)} %bitcast.125, pred[8,63,8,256]{3,1,2,0:T(8,128)(4,1)} %fusion.3), kind=kOutput, calls=%fused_computation.23 | convolution fusion | flops 1587511296 | bytes 13451264 | tf_op jit(solution)/shard_map/slmd,dlt->slmt/dot_general | solution.py:223
  107.3 0.0 all-reduce.4.cloned.1.call-update
  107.4 1.1 select_select_fusion
  108.5 1.3 select_reduce_fusion.2
  109.8 0.8 copy.46
  110.6 48.7 %all-reduce.4.cloned.1.call-done = f32[8,63,8,128]{3,2,0,1:T(8,128)} async-done(((f32[8,63,8,128]{3,2,0,1:T(8,128)}), f32[8,63,8,128]{3,2,0,1:T(8,128)}) %all-reduce.4.cloned.1.call-update) | async-done | bytes 2064400 | tf_op jit(solution)/shard_map/psum | solution.py:226
  159.3 2.9 %reduce_max.46 = f32[8,63,8]{2,0,1:T(8,128)} reduce(f32[8,63,8,128]{3,2,0,1:T(8,128)} %all-reduce.4.cloned.1.call-done, f32[]{:T(128)} %constant.8.clone.1), dimensions={3}, to_apply=%region_7.8 | reduce | flops 512064 | bytes 2080516 | tf_op jit(solution)/shard_map/reduce_max | solution.py:227
  162.2 1.1 copy.43
  163.3 1.0 select_reduce_fusion.5
  164.3 0.9 select_reduce_fusion.4
  165.2 0.9 copy.44
  166.1 4.8 %exponential_reduce_fusion = (f32[8,63,8]{2,0,1:T(8,128)}, f32[8,63,8]{2,0,1:T(8,128)}) fusion(f32[8,63,8,128]{3,2,0,1:T(8,128)} %all-reduce.4.cloned.1.call-done, f32[8,63,8]{2,0,1:T(8,128)} %copy.44, s32[8,63,8]{2,0,1:T(8,128)} %copy.46), kind=kLoop, calls=%fused_computation.22 | loop fusion | flops 2572416 | bytes 2128896 | tf_op jit(solution)/shard_map/reduce_sum | solution.py:230
  170.8 1.1 copy.45
  171.9 1.1 copy.47
  173.0 1.5 select_reduce_fusion.3
  174.5 8.8 %shard_map.133 = f32[8,3,8,256]{3,2,1,0:T(8,128)S(1)} custom-call(f32[3,8,256]{2,1,0:T(8,128)S(1)} %pad_maximum_fusion.own_ref), custom_call_target="tpu_custom_call" | custom-call | tf_op jit(solution)/shard_map/pallas_call | solution.py:59
  183.4 0.9 select_reduce_fusion
  184.3 0.9 copy.49
  185.1 6.4 %convert_bitcast_fusion = bf16[8,63,8,512]{3,2,0,1:T(8,128)(2,1)S(1)} fusion(bf16[512,63,128,1]{0,2,3,1:T(8,128)(2,1)} %bitcast.124, f32[8,63,8,128]{3,2,0,1:T(8,128)} %all-reduce.4.cloned.1.call-done, f32[8,63,8]{2,0,1:T(8,128)} %copy.49, s32[8,63,8]{2,0,1:T(8,128)} %copy.46), kind=kOutput, calls=%fused_computation.13 | convolution fusion | flops 533127168 | bytes 14482944 | tf_op jit(solution)/shard_map/slmt,dlt->slmd/dot_general | solution.py:246
  191.6 6.5 %bitcast_convert_fusion = bf16[8,256,512]{2,1,0:T(8,128)(2,1)} fusion(bf16[8,63,8,512]{3,2,0,1:T(8,128)(2,1)S(1)} %convert_bitcast_fusion, s32[8,63,256]{2,1,0:T(8,128)S(1)} %convolution_convert_fusion, pred[8,63,256]{2,1,0:T(8,128)(4,1)S(1)} %fusion.29), kind=kOutput, calls=%fused_computation.1 | convolution fusion | flops 1060077568 | bytes 6871040 | tf_op jit(solution)/shard_map/slmr,slmd->srd/dot_general | solution.py:249
  198.1 4.4 %all-to-all-start = ((bf16[8,256,512]{2,1,0:T(8,128)(2,1)}), bf16[8,256,512]{2,1,0:T(8,128)(2,1)}, u32[]{:S(2)}, u32[]{:S(2)}) async-start(bf16[8,256,512]{2,1,0:T(8,128)(2,1)} %bitcast_convert_fusion), calls=%async_computation | async-start | bytes 4194304 | tf_op jit(solution)/shard_map/all_to_all | solution.py:252
  202.6 0.6 dynamic-slice_subtract_fusion
  203.1 44.9 %all-to-all-done = bf16[8,256,512]{2,1,0:T(8,128)(2,1)} async-done(((bf16[8,256,512]{2,1,0:T(8,128)(2,1)}), bf16[8,256,512]{2,1,0:T(8,128)(2,1)}, u32[]{:S(2)}, u32[]{:S(2)}) %all-to-all-start) | async-done | bytes 2097184 | tf_op jit(solution)/shard_map/all_to_all | solution.py:252
  248.0 2.7 %convert_reduce_fusion = f32[256,512]{1,0:T(8,128)} fusion(bf16[8,256,512]{2,1,0:T(8,128)(2,1)} %all-to-all-done), kind=kLoop, calls=%fused_computation.4 | loop fusion | flops 1966080 | bytes 2621440 | tf_op jit(solution)/shard_map/reduce_sum | solution.py:253
  250.7 1.2 copy.52
  252.0 0.2 multiply_reduce_fusion.2
  252.2 5.5 %all-reduce = (f32[256]{0:T(256)S(1)}, f32[256]{0:T(256)S(1)}) all-reduce(f32[256]{0:T(256)S(1)} %get-tuple-element.15, f32[256]{0:T(256)S(1)} %get-tuple-element.14), channel_id=1, replica_groups=mesh['src'=4,'vocab'=8] {'src'}, use_global_device_ids=true, to_apply=%region_23.24 | all-reduce | flops 512 | bytes 4096 | tf_op jit(solution)/shard_map/psum | solution.py:255
  257.7 1.0 subtract_multiply_fusion
  258.6 2.0 copy.53
  (32 shorter events, 0.2 us)
Async XLA Ops:
  7.2 7.9 %copy-start = (bf16[512,2048]{1,0:T(8,128)(2,1)S(1)}, bf16[512,2048]{1,0:T(8,128)(2,1)}, u32[]{:S(2)}) copy-start(bf16[512,2048]{1,0:T(8,128)(2,1)} %param.16) | copy-start | bytes 6291460
  7.2 5.6 %copy-start.4 = (bf16[256,512]{1,0:T(8,128)(2,1)S(1)}, bf16[256,512]{1,0:T(8,128)(2,1)}, u32[]{:S(2)}) copy-start(bf16[256,512]{1,0:T(8,128)(2,1)} %param.17) | copy-start | bytes 786436
  7.2 5.7 %copy-start.5 = (bf16[1,256,512]{2,1,0:T(8,128)(2,1)S(1)}, bf16[1,256,512]{2,1,0:T(8,128)(2,1)}, u32[]{:S(2)}) copy-start(bf16[1,256,512]{2,1,0:T(8,128)(2,1)} %param.14) | copy-start | bytes 786436
  7.2 87.2 %all-gather.3.cloned.1.call-start = ((), (), s32[]{:S(2)}) async-start(), calls=%async_computation.2 | async-start | bytes 2359296 | tf_op jit(solution)/shard_map/all_gather | solution.py:218
  12.9 30.8 %copy-start.2 = (bf16[256,512]{0,1:T(8,128)(2,1)}, bf16[256,512]{0,1:T(8,128)(2,1)S(1)}, u32[]{:S(2)}) copy-start(bf16[256,512]{0,1:T(8,128)(2,1)S(1)} %copy.33) | copy-start | bytes 786436
  17.1 26.6 %copy-start.6 = (f32[512]{0:T(512)S(1)}, f32[512]{0:T(512)}, u32[]{:S(2)}) copy-start(f32[512]{0:T(512)} %param.18) | copy-start | bytes 6148
  17.1 26.6 %copy-start.8 = (f32[512]{0:T(512)S(1)}, f32[512]{0:T(512)}, u32[]{:S(2)}) copy-start(f32[512]{0:T(512)} %param.19) | copy-start | bytes 6148
  17.1 27.8 %copy-start.7 = (s32[256,8]{0,1:T(8,128)S(1)}, s32[256,8]{0,1:T(8,128)}, u32[]{:S(2)}) copy-start(s32[256,8]{0,1:T(8,128)} %param.21) | copy-start | bytes 24580
  17.1 27.8 %copy-start.9 = (s32[256]{0:T(256)S(1)}, s32[256]{0:T(256)}, u32[]{:S(2)}) copy-start(s32[256]{0:T(256)} %param.23) | copy-start | bytes 3076
  17.1 27.8 %copy-start.10 = (s32[256]{0:T(256)S(1)}, s32[256]{0:T(256)}, u32[]{:S(2)}) copy-start(s32[256]{0:T(256)} %param.22) | copy-start | bytes 3076
  20.1 1.6 copy-start.1
  44.7 114.7 %all-reduce.4.cloned.1.call-start = ((), (), s32[]{:S(2)}) async-start(), calls=%async_computation.1 | async-start | bytes 4128768 | tf_op jit(solution)/shard_map/psum | solution.py:226
  198.1 53.9 %copy-start.3 = (bf16[256,512]{0,1:T(8,128)(2,1)S(1)}, bf16[256,512]{0,1:T(8,128)(2,1)}, u32[]{:S(2)}) copy-start(bf16[256,512]{0,1:T(8,128)(2,1)} %copy-done.2) | copy-start | bytes 786436
  198.1 49.9 %all-to-all-start = ((bf16[8,256,512]{2,1,0:T(8,128)(2,1)}), bf16[8,256,512]{2,1,0:T(8,128)(2,1)}, u32[]{:S(2)}, u32[]{:S(2)}) async-start(bf16[8,256,512]{2,1,0:T(8,128)(2,1)} %bitcast_convert_fusion), calls=%async_computation | async-start | bytes 4194304 | tf_op jit(solution)/shard_map/all_to_all | solution.py:252
Sparse Core Ops, SparseCore 0:
  44.8 49.5 all-gather.2
  107.5 51.8 all-reduce.3

commit v3 on v2

--- a/solution.py
+++ b/solution.py
@@ -59,6 +59,39 @@
     return pl.pallas_call(
         functools.partial(gather_body, axis, count),
         out_shape=jax.ShapeDtypeStruct((count,) + own.shape, own.dtype),
+        in_specs=[pl.BlockSpec(memory_space=pltpu.VMEM)],
+        out_specs=pl.BlockSpec(memory_space=pltpu.VMEM),
+        scratch_shapes=[
+            pltpu.SemaphoreType.DMA((count - 1,)),
+            pltpu.SemaphoreType.DMA((count - 1,)),
+        ],
+        compiler_params=pltpu.CompilerParams(
+            collective_id=collective_id, has_side_effects=True, vmem_limit_bytes=VMEM_BYTES
+        ),
+    )(own)
+
+
+def exchange_body(axis, count, own_ref, all_ref, send_sems, recv_sems):
+    me = lax.axis_index(axis)
+    partners = [lax.rem(me + step, count) for step in range(1, count)]
+    greet(axis, partners)
+    copies = []
+    for i, partner in enumerate(partners):
+        copy = remote(
+            axis, own_ref.at[partner], all_ref.at[me], send_sems.at[i], recv_sems.at[i], partner
+        )
+        copy.start()
+        copies.append(copy)
+    all_ref[me] = own_ref[me]
+    for copy in copies:
+        copy.wait()
+
+
+def exchange(own, axis, collective_id):
+    count = lax.axis_size(axis)
+    return pl.pallas_call(
+        functools.partial(exchange_body, axis, count),
+        out_shape=jax.ShapeDtypeStruct(own.shape, own.dtype),
         in_specs=[pl.BlockSpec(memory_space=pltpu.VMEM)],
         out_specs=pl.BlockSpec(memory_space=pltpu.VMEM),
         scratch_shapes=[
@@ -249,7 +282,7 @@
     grad_rows = jnp.einsum(
         "slmr,slmd->srd", places, grad_slots, preferred_element_type=jnp.float32
     ).astype(jnp.bfloat16)
-    returned = lax.all_to_all(grad_rows, "vocab", split_axis=0, concat_axis=0, tiled=True)
+    returned = exchange(grad_rows, "vocab", 4)
     grad_normed = jnp.sum(returned.astype(jnp.float32), axis=0)
     gained = grad_normed * norm_gain
     sum_g, sum_gx = lax.psum((jnp.sum(gained, axis=1), jnp.sum(gained * centered, axis=1)), "src")

time: 273 us -> 271 us (level); the launches traced: 268 us -> 270 us
  waiting for transfers between devices: 122 us -> 68.6 us
  Pallas kernels: 31.4 us -> 79.1 us
  local copies, waits for them, and re-layouts: 30.7 us -> 39.5 us
  starting transfers between devices: 4.7 us -> 0.26 us
  other arithmetic: 22.1 us -> 25.9 us
    pallas_call x0 -> x1, Pallas kernels: none -> 47.7 us  [exchange(): pl.pallas_call(functools.partial(exchange_body, axis, count), out_shape=j...]
    all_to_all x1 -> x0, waiting for transfers between devices: 44.9 us -> none  [shards(): lax.all_to_all(grad_rows, 'vocab', split_axis=0, concat_axis=0, tiled=True)]
    psum x1, waiting for transfers between devices: 48.7 us -> 41.7 us  [shards(): full_logits = lax.psum(partial_logits, 'src')]
    all_to_all x1 -> x0, starting transfers between devices: 4.44 us -> none  [shards(): lax.all_to_all(grad_rows, 'vocab', split_axis=0, concat_axis=0, tiled=True)]
    unnamed x34 -> x56, local copies, waits for them, and re-layouts: 15.6 us -> 19.8 us
  transfers between devices with their start and end apart: 3 -> 2, of which waited for: 3 -> 2; matrix products, arithmetic and copies ran while one was open for 7% -> 10% of each run, Pallas kernels for 2% -> 2%
where the time goes in v3:
time: 271 us; the launch traced here: 270 us
  Pallas kernels  79.1 us (29%)
  waiting for transfers between devices  68.6 us (25%)
  local copies, waits for them, and re-layouts  39.5 us (15%)
  matrix products  29 us (11%)
  other arithmetic  25.9 us (10%)
  between operations  15.3 us (6%)
  blocking collectives  12.1 us (4%)
    pallas_call x1, Pallas kernels, exchange(): pl.pallas_call(functools.partial(exchange_body, axis, count), out_shape=j...  47.7 us
    psum x1, waiting for transfers between devices, shards(): full_logits = lax.psum(partial_logits, 'src')  41.7 us
    all_gather x1, waiting for transfers between devices, shards(): normed_all = lax.all_gather(normed, 'vocab', axis=0)  26.9 us
    unnamed x56, local copies, waits for them, and re-layouts  19.8 us
    pallas_call x1, Pallas kernels, scatter_sum(): pl.pallas_call(functools.partial(scatter_body, axis, rings), out_shape=ja...  16.3 us
    pallas_call x2, Pallas kernels, gather_small(): pl.pallas_call(functools.partial(gather_body, axis, count), out_shape=jax...  15.2 us
    dot_general x1, matrix products, shards(): jnp.einsum('slmd,dlt->slmt', received, weight_view, preferred_element_typ...  9.03 us
    psum x1, blocking collectives, shards(): lax.psum((jnp.sum(gained, axis=1), jnp.sum(gained * centered, axis=1)), '...  6.49 us
  transfers between devices with their start and end apart: 2, of which 2 were waited for; matrix products, arithmetic and copies ran while one was open for 10% of the time, Pallas kernels for 2%

profile of v3, /device:TPU:11, one launch (start us, length us, event | category | flops | bytes accessed | tf_op | source)
XLA Modules:
  0.0 269.8 jit_solution(17256087767085266684)
XLA Ops:
  7.2 0.0 copy-start
  7.2 0.0 all-gather.3.cloned.1.call-start
  8.1 1.0 reshape_squeeze.6
  9.1 1.5 fusion.63
  10.5 2.2 fusion.22
  12.8 0.1 copy.33
  12.9 0.1 copy.58
  13.1 1.9 fusion.24
  15.0 2.1 convolution_bitcast_fusion
  17.1 2.9 %copy.38 = f32[2048,256]{1,0:T(8,128)} copy(f32[2048,256]{0,1:T(8,128)} %convolution_bitcast_fusion) | data formatting | bytes 4194304 | tf_op jit(solution)/shard_map/dot_general | solution.py:211
  20.1 1.6 copy-done.1
  21.7 16.3 %shard_map.132 = f32[512,256]{1,0:T(8,128)S(1)} custom-call(f32[4,512,256]{2,1,0:T(8,128)S(1)} %bitcast.122), custom_call_target="tpu_custom_call" | custom-call | tf_op jit(solution)/shard_map/pallas_call | solution.py:150
  38.0 0.1 fusion.59
  38.1 5.6 %all-reduce.1 = (f32[256]{0:T(256)S(1)}, f32[256]{0:T(256)S(1)}) all-reduce(f32[256]{0:T(256)S(1)} %get-tuple-element.11, f32[256]{0:T(256)S(1)} %get-tuple-element.10), channel_id=1, replica_groups=mesh['src'=4,'vocab'=8] {'src'}, use_global_device_ids=true, to_apply=%region_5.6 | all-reduce | flops 512 | bytes 4096 | tf_op jit(solution)/shard_map/psum | solution.py:218
  43.7 0.9 add_convert_fusion
  44.6 0.0 all-gather.3.cloned.1.call-update
  44.7 0.2 all-reduce.4.cloned.1.call-start
  44.9 6.3 %shard_map.131 = s32[8,10,256]{2,1,0:T(8,128)S(1)} custom-call(s32[10,256]{1,0:T(8,128)S(1)} %pad_add_fusion.own_ref), custom_call_target="tpu_custom_call" | custom-call | tf_op jit(solution)/shard_map/pallas_call | solution.py:59
  51.3 11.8 %copy.41 = bf16[512,8064]{0,1:T(8,128)(2,1)} copy(bf16[512,8064]{1,0:T(8,128)(2,1)} %param.20) | data formatting | bytes 16515072 | tf_op args[8]
  63.1 0.7 broadcast_compare_fusion.7
  63.8 0.5 copy_bitcast_fusion.15
  64.5 0.5 fusion.29
  65.0 0.0 copy-done.6
  65.0 0.0 copy-done.8
  65.1 0.0 copy-done.10
  65.1 0.0 copy-done.11
  65.1 0.6 convolution_convert_fusion
  65.7 0.0 copy-done.2
  65.8 1.8 fusion.3
  67.5 26.9 %all-gather.3.cloned.1.call-done = bf16[2048,512]{0,1:T(8,128)(2,1)} async-done(((bf16[256,512]{0,1:T(8,128)(2,1)}), bf16[2048,512]{0,1:T(8,128)(2,1)}) %all-gather.3.cloned.1.call-update) | async-done | bytes 2097168 | tf_op jit(solution)/shard_map/all_gather | solution.py:251
  94.4 3.9 %copy.59 = bf16[2048,512]{1,0:T(8,128)(2,1)} copy(bf16[2048,512]{0,1:T(8,128)(2,1)} %all-gather.3.cloned.1.call-done) | data formatting | bytes 4194304 | tf_op jit(solution)/shard_map/all_gather | solution.py:251
  98.3 9.0 %fusion.14 = f32[8,63,8,128]{3,2,0,1:T(8,128)} fusion(bf16[512,63,128,1]{0,2,3,1:T(8,128)(2,1)} %bitcast.123, bf16[8,256,512,1]{2,1,0,3:T(8,128)(2,1)} %bitcast.125, pred[8,63,8,256]{3,1,2,0:T(8,128)(4,1)} %fusion.3), kind=kOutput, calls=%fused_computation.23 | convolution fusion | flops 1587511296 | bytes 13451264 | tf_op jit(solution)/shard_map/slmd,dlt->slmt/dot_general | solution.py:256
  107.3 0.0 all-reduce.4.cloned.1.call-update
  107.3 1.3 copy_bitcast_fusion.13
  108.6 0.6 slice.67
  109.2 0.7 copy.126
  109.9 0.7 copy_bitcast_fusion.11
  110.7 0.7 copy_bitcast_fusion.9
  111.4 1.9 select_select_fusion
  113.2 2.8 %select_reduce_fusion.2 = s32[8,63,8]{1,2,0:T(8,128)} fusion(s32[8,63,256]{2,1,0:T(8,128)S(1)} %select_select_fusion, s32[8,63,256]{2,1,0:T(8,128)S(1)} %convolution_convert_fusion, pred[8,63,256]{2,1,0:T(8,128)(4,1)} %copy-done.2), kind=kLoop, calls=%fused_computation.7 | loop fusion | flops 4124736 | bytes 1177344 | tf_op jit(solution)/shard_map/reduce_max | solution.py:250
  116.0 1.6 copy.46
  117.6 41.7 %all-reduce.4.cloned.1.call-done = f32[8,63,8,128]{3,2,0,1:T(8,128)} async-done(((f32[8,63,8,128]{3,2,0,1:T(8,128)}), f32[8,63,8,128]{3,2,0,1:T(8,128)}) %all-reduce.4.cloned.1.call-update) | async-done | bytes 2064400 | tf_op jit(solution)/shard_map/psum | solution.py:259
  159.3 2.9 %reduce_max.46 = f32[8,63,8]{2,0,1:T(8,128)} reduce(f32[8,63,8,128]{3,2,0,1:T(8,128)} %all-reduce.4.cloned.1.call-done, f32[]{:T(128)} %constant.8.clone.1), dimensions={3}, to_apply=%region_7.8 | reduce | flops 512064 | bytes 2080516 | tf_op jit(solution)/shard_map/reduce_max | solution.py:260
  162.2 1.7 copy.43
  163.9 1.7 select_reduce_fusion.5
  165.6 1.5 select_reduce_fusion.4
  167.1 1.6 copy.44
  168.7 4.8 %exponential_reduce_fusion = (f32[8,63,8]{2,0,1:T(8,128)}, f32[8,63,8]{2,0,1:T(8,128)}) fusion(f32[8,63,8,128]{3,2,0,1:T(8,128)} %all-reduce.4.cloned.1.call-done, f32[8,63,8]{2,0,1:T(8,128)} %copy.44, s32[8,63,8]{2,0,1:T(8,128)} %copy.46), kind=kLoop, calls=%fused_computation.22 | loop fusion | flops 2572416 | bytes 2128896 | tf_op jit(solution)/shard_map/reduce_sum | solution.py:263
  173.5 1.7 copy.45
  175.2 1.7 copy.47
  176.9 2.0 select_reduce_fusion.3
  178.9 8.8 %shard_map.133 = f32[8,3,8,256]{3,2,1,0:T(8,128)S(1)} custom-call(f32[3,8,256]{2,1,0:T(8,128)S(1)} %pad_maximum_fusion.own_ref), custom_call_target="tpu_custom_call" | custom-call | tf_op jit(solution)/shard_map/pallas_call | solution.py:59
  187.8 1.5 select_reduce_fusion
  189.4 1.6 copy.49
  191.0 6.4 %convert_bitcast_fusion = bf16[8,63,8,512]{3,2,0,1:T(8,128)(2,1)S(1)} fusion(bf16[512,63,128,1]{0,2,3,1:T(8,128)(2,1)} %bitcast.124, f32[8,63,8,128]{3,2,0,1:T(8,128)} %all-reduce.4.cloned.1.call-done, f32[8,63,8]{2,0,1:T(8,128)} %copy.49, s32[8,63,8]{2,0,1:T(8,128)} %copy.46), kind=kOutput, calls=%fused_computation.13 | convolution fusion | flops 533127168 | bytes 14482944 | tf_op jit(solution)/shard_map/slmt,dlt->slmd/dot_general | solution.py:279
  197.4 5.2 %bitcast_convert_fusion.own_ref = bf16[8,256,512]{2,1,0:T(8,128)(2,1)S(1)} fusion(bf16[8,63,8,512]{3,2,0,1:T(8,128)(2,1)S(1)} %convert_bitcast_fusion, s32[8,63,256]{2,1,0:T(8,128)S(1)} %convolution_convert_fusion, pred[8,63,256]{2,1,0:T(8,128)(4,1)S(1)} %copy-done.3), kind=kOutput, calls=%fused_computation.1 | convolution fusion | flops 1060077568 | bytes 6871040 | tf_op jit(solution)/shard_map/slmr,slmd->srd/dot_general | solution.py:282
  202.7 47.7 %shard_map.134 = bf16[8,256,512]{2,1,0:T(8,128)(2,1)S(1)} custom-call(bf16[8,256,512]{2,1,0:T(8,128)(2,1)S(1)} %bitcast_convert_fusion.own_ref), custom_call_target="tpu_custom_call" | custom-call | tf_op jit(solution)/shard_map/pallas_call | solution.py:92
  250.3 1.1 convert_reduce_fusion
  251.4 1.2 copy.52
  252.7 0.2 multiply_reduce_fusion.2
  252.9 6.5 %all-reduce = (f32[256]{0:T(256)S(1)}, f32[256]{0:T(256)S(1)}) all-reduce(f32[256]{0:T(256)S(1)} %get-tuple-element.15, f32[256]{0:T(256)S(1)} %get-tuple-element.14), channel_id=1, replica_groups=mesh['src'=4,'vocab'=8] {'src'}, use_global_device_ids=true, to_apply=%region_23.24 | all-reduce | flops 512 | bytes 4096 | tf_op jit(solution)/shard_map/psum | solution.py:288
  259.4 1.0 subtract_multiply_fusion
  260.3 2.0 copy.53
  262.4 0.6 dynamic-slice_subtract_fusion
  (53 shorter events, 0.2 us)
Async XLA Ops:
  7.2 7.9 %copy-start = (bf16[512,2048]{1,0:T(8,128)(2,1)S(1)}, bf16[512,2048]{1,0:T(8,128)(2,1)}, u32[]{:S(2)}) copy-start(bf16[512,2048]{1,0:T(8,128)(2,1)} %param.16) | copy-start | bytes 6291460
  7.2 5.6 %copy-start.4 = (bf16[256,512]{1,0:T(8,128)(2,1)S(1)}, bf16[256,512]{1,0:T(8,128)(2,1)}, u32[]{:S(2)}) copy-start(bf16[256,512]{1,0:T(8,128)(2,1)} %param.17) | copy-start | bytes 786436
  7.2 5.7 %copy-start.5 = (bf16[1,256,512]{2,1,0:T(8,128)(2,1)S(1)}, bf16[1,256,512]{2,1,0:T(8,128)(2,1)}, u32[]{:S(2)}) copy-start(bf16[1,256,512]{2,1,0:T(8,128)(2,1)} %param.14) | copy-start | bytes 786436
  7.2 87.2 %all-gather.3.cloned.1.call-start = ((), (), s32[]{:S(2)}) async-start(), calls=%async_computation.1 | async-start | bytes 2359296 | tf_op jit(solution)/shard_map/all_gather | solution.py:251
  17.1 26.6 %copy-start.12 = (f32[512]{0:T(512)S(1)}, f32[512]{0:T(512)}, u32[]{:S(2)}) copy-start(f32[512]{0:T(512)} %param.18) | copy-start | bytes 6148
  17.1 26.6 %copy-start.19 = (f32[512]{0:T(512)S(1)}, f32[512]{0:T(512)}, u32[]{:S(2)}) copy-start(f32[512]{0:T(512)} %param.19) | copy-start | bytes 6148
  17.1 27.8 %copy-start.18 = (s32[256,8]{0,1:T(8,128)S(1)}, s32[256,8]{0,1:T(8,128)}, u32[]{:S(2)}) copy-start(s32[256,8]{0,1:T(8,128)} %param.21) | copy-start | bytes 24580
  17.1 27.8 %copy-start.20 = (s32[256]{0:T(256)S(1)}, s32[256]{0:T(256)}, u32[]{:S(2)}) copy-start(s32[256]{0:T(256)} %param.23) | copy-start | bytes 3076
  17.1 27.8 %copy-start.21 = (s32[256]{0:T(256)S(1)}, s32[256]{0:T(256)}, u32[]{:S(2)}) copy-start(s32[256]{0:T(256)} %param.22) | copy-start | bytes 3076
  20.1 1.6 copy-start.1
  43.7 19.4 %copy-start.14 = (f32[256]{0:T(256)}, f32[256]{0:T(256)S(1)}, u32[]{:S(2)}) copy-start(f32[256]{0:T(256)S(1)} %get-tuple-element.36) | copy-start | bytes 3076
  43.7 19.4 %copy-start.16 = (f32[256]{0:T(256)}, f32[256]{0:T(256)S(1)}, u32[]{:S(2)}) copy-start(f32[256]{0:T(256)S(1)} %get-tuple-element.37) | copy-start | bytes 3076
  44.7 114.7 %all-reduce.4.cloned.1.call-start = ((), (), s32[]{:S(2)}) async-start(), calls=%async_computation | async-start | bytes 4128768 | tf_op jit(solution)/shard_map/psum | solution.py:259
  64.4 0.6 copy-start.6
  64.4 0.6 copy-start.7
  64.5 0.6 copy-start.8
  64.5 0.6 copy-start.9
  64.5 0.6 copy-start.10
  64.5 0.6 copy-start.11
  65.1 0.7 copy-start.2
  109.2 54.7 %copy-start.3 = (pred[8,63,256]{2,1,0:T(8,128)(4,1)S(1)}, pred[8,63,256]{2,1,0:T(8,128)(4,1)}, u32[]{:S(2)}) copy-start(pred[8,63,256]{2,1,0:T(8,128)(4,1)} %copy-done.2) | copy-start | bytes 387076
  202.6 50.1 %copy-start.13 = (f32[512]{0:T(512)S(1)}, f32[512]{0:T(512)}, u32[]{:S(2)}) copy-start(f32[512]{0:T(512)} %param.18) | copy-start | bytes 6148
  202.6 50.1 %copy-start.15 = (f32[256]{0:T(256)S(1)}, f32[256]{0:T(256)}, u32[]{:S(2)}) copy-start(f32[256]{0:T(256)} %copy-done.14) | copy-start | bytes 3076
  202.6 50.1 %copy-start.17 = (f32[256]{0:T(256)S(1)}, f32[256]{0:T(256)}, u32[]{:S(2)}) copy-start(f32[256]{0:T(256)} %copy-done.16) | copy-start | bytes 3076
Sparse Core Ops, SparseCore 0:
  44.8 49.5 all-gather.2
  107.5 51.8 all-reduce.3
